TPU v7x, 768 devices: a whole 4x8x12 slice. The times are simulated.
768 devices in a mesh: wide: 96 (over y, z), narrow: 8 (over x, core).
Axes of the slice: x: 4, y: 8, z: 12, core: 2. Of those that a mesh axis runs over, the one named last changes fastest.
Arguments:
- tile_values: bfloat16 [98304, 128, 128], P(('wide', 'narrow')), may hold values from -6 to 6
- tile_row: int32 [98304], P(('wide', 'narrow')), may hold values from 0 to 15
- tile_col: int32 [98304], P(('wide', 'narrow')), may hold values from 0 to 23
- tile_count: int32 [768], P(('wide', 'narrow')), may hold values from 32 to 128, as said below
- user_degree: int32 [196608], P('wide'), may hold values from 16 to 3968
- item_degree: int32 [24576], P('narrow'), may hold values from 16 to 3968
- start_vectors: float32 [64, 24576], P(None, 'narrow'), may hold values from -6 to 6
Outputs:
- user_vectors: float32 [64, 196608], P(None, 'wide')
- item_vectors: float32 [64, 24576], P(None, 'narrow')
Inputs may be any that keep to these rules, and one draw needn't show every extreme that they name: `tile_count`: each device's used slots are its first ones; some device uses all 128.
All inputs are finite; a program needn't handle non-finite values.
Results may differ from a plain program's by a relative error of at most 0.0041.
Values sent between devices are 32-bit elements; how exact they have to be, the bound alone decides.
No kernel may reach another device: no remote copies, remote signals or barrier semaphores. Data moves between devices by JAX's collectives and lax.ppermute only.
A program may use at most 32 MiB of HBM per device.

v0:
```python
import jax
import jax.numpy as jnp
from jax import lax
from jax.sharding import PartitionSpec as P

ITERS = 2


def block_terms(tile_values, source_blocks, pick_index, target_onehot, forward):
    picked = jnp.take(source_blocks, pick_index, axis=1)
    if forward:
        products = jnp.einsum(
            "ktc,trc->ktr", picked, tile_values, preferred_element_type=jnp.float32
        )
    else:
        products = jnp.einsum(
            "ktr,trc->ktc", picked, tile_values, preferred_element_type=jnp.float32
        )
    return jnp.einsum("tb,ktr->kbr", target_onehot, products, precision=lax.Precision.HIGHEST)


def local(tile_values, tile_row, tile_col, tile_count, user_degree, item_degree, start_vectors):
    vectors, item_rows = start_vectors.shape
    slot_count = tile_values.shape[0]
    tile_size = tile_values.shape[1]
    user_rows = user_degree.shape[0]
    user_blocks = user_rows // tile_size
    item_blocks = item_rows // tile_size
    wide_count = lax.axis_size("wide")
    narrow_count = lax.axis_size("narrow")
    all_users = user_rows * wide_count
    all_items = item_rows * narrow_count
    user_scale = lax.rsqrt(user_degree.astype(jnp.float32))
    item_scale = lax.rsqrt(item_degree.astype(jnp.float32))
    in_use = (jnp.arange(slot_count) < tile_count[0]).astype(jnp.float32)
    user_onehot = (tile_row[:, None] == jnp.arange(user_blocks)[None, :]).astype(
        jnp.float32
    ) * in_use[:, None]
    item_onehot = (tile_col[:, None] == jnp.arange(item_blocks)[None, :]).astype(
        jnp.float32
    ) * in_use[:, None]

    def products(source_blocks, pick_index, target_onehot, forward):
        return block_terms(tile_values, source_blocks, pick_index, target_onehot, forward)

    item_vectors = start_vectors
    user_vectors = start_vectors
    for step in range(ITERS):
        scaled_items = (item_vectors * item_scale[None, :]).astype(jnp.bfloat16)
        user_terms = products(
            scaled_items.reshape(vectors, item_blocks, tile_size), tile_col, user_onehot, True
        )
        user_sums = lax.psum(user_terms.reshape(vectors, user_rows), "narrow")
        user_raw = user_sums * user_scale[None, :]
        local_gram = jnp.dot(user_raw, user_raw.T, precision=lax.Precision.HIGHEST)
        user_gram = lax.psum(local_gram, "wide") / all_users
        factor = jnp.linalg.cholesky(user_gram)
        user_vectors = jax.scipy.linalg.solve_triangular(factor, user_raw, lower=True)
        scaled_users = (user_vectors * user_scale[None, :]).astype(jnp.bfloat16)
        item_terms = products(
            scaled_users.reshape(vectors, user_blocks, tile_size), tile_row, item_onehot, False
        )
        item_terms = item_terms.reshape(vectors, item_rows)
        item_sums = lax.psum(item_terms, "wide")
        item_raw = item_sums * item_scale[None, :]
        block_gram = jnp.dot(item_raw, item_raw.T, precision=lax.Precision.HIGHEST)
        item_gram = lax.psum(block_gram, "narrow") / all_items
        factor_two = jnp.linalg.cholesky(item_gram)
        item_vectors = jax.scipy.linalg.solve_triangular(factor_two, item_raw, lower=True)
    return (user_vectors, item_vectors)


def solution(mesh):
    return jax.shard_map(
        local,
        mesh=mesh,
        in_specs=(
            P(("wide", "narrow"), None, None),
            P(("wide", "narrow")),
            P(("wide", "narrow")),
            P(("wide", "narrow")),
            P("wide"),
            P("narrow"),
            P(None, "narrow"),
        ),
        out_specs=(P(None, "wide"), P(None, "narrow")),
        check_vma=False,
    )
```

profile of v0, /device:TPU:1, one launch (start us, length us, event | category | flops | bytes accessed | tf_op | source)
XLA Modules:
  0.0 1605.2 jit_solution(11994957261672157459)
XLA Ops:
  7.2 0.7 compare_and_fusion
  7.9 0.7 compare_select_fusion
  9.2 0.7 convert_rsqrt_fusion
  9.9 1.2 copy_bitcast_fusion.5
  11.2 1.0 gather_fusion
  12.1 5.1 fusion.20
  17.3 4.6 fusion.6
  21.9 1.0 copy.72
  23.0 83.7 %all-reduce.5.cloned.1.call-done = f32[64,2048]{1,0:T(8,128)} async-done(((f32[64,2048]{1,0:T(8,128)}), f32[64,2048]{1,0:T(8,128)}) %all-reduce.5.cloned.1.call-update) | async-done | bytes 524304 | tf_op jit(solution)/shard_map/psum | solution.py:53
  106.7 1.8 fusion.48
  108.5 334.3 %psum.57 = f32[64,64]{0,1:T(8,128)S(1)} all-reduce(f32[64,64]{0,1:T(8,128)S(1)} %fusion.48), channel_id=1, replica_groups=mesh['wide'=96,'narrow'=8] {'wide'}, use_global_device_ids=true, to_apply=%region_1.3 | all-reduce | flops 4096 | bytes 32768 | tf_op jit(solution)/shard_map/psum | solution.py:56
  442.9 5.8 cholesky.74
  449.4 0.7 fusion.60
  450.1 4.9 custom-call.10
  455.0 1.7 fusion.31
  456.7 1.0 gather_fusion.1
  457.7 3.5 fusion.18
  461.2 4.6 fusion.4
  465.8 1.0 copy.70
  466.9 298.6 %all-reduce.7.cloned.1.call-done = f32[64,3072]{1,0:T(8,128)} async-done(((f32[64,3072]{1,0:T(8,128)}), f32[64,3072]{1,0:T(8,128)}) %all-reduce.7.cloned.1.call-update) | async-done | bytes 786448 | tf_op jit(solution)/shard_map/psum | solution.py:64
  765.5 2.2 fusion.41
  767.7 27.7 %psum.59 = f32[64,64]{0,1:T(8,128)S(1)} all-reduce(f32[64,64]{0,1:T(8,128)S(1)} %fusion.41), channel_id=1, replica_groups=mesh['wide'=96,'narrow'=8] {'narrow'}, use_global_device_ids=true, to_apply=%region_5.10 | all-reduce | flops 4096 | bytes 32768 | tf_op jit(solution)/shard_map/psum | solution.py:67
  795.5 5.8 cholesky.85
  802.0 0.7 fusion.61
  802.7 4.9 custom-call.11
  807.6 2.0 fusion.30
  809.7 1.0 gather_fusion.2
  810.6 5.1 fusion.16
  815.8 4.6 fusion.2
  820.4 1.0 copy.71
  821.4 73.4 %all-reduce.9.cloned.1.call-done = f32[64,2048]{1,0:T(8,128)} async-done(((f32[64,2048]{1,0:T(8,128)}), f32[64,2048]{1,0:T(8,128)}) %all-reduce.9.cloned.1.call-update) | async-done | bytes 524304 | tf_op jit(solution)/shard_map/psum | solution.py:53
  894.8 1.8 fusion.45
  896.6 334.0 %psum.61 = f32[64,64]{0,1:T(8,128)S(1)} all-reduce(f32[64,64]{0,1:T(8,128)S(1)} %fusion.45), channel_id=1, replica_groups=mesh['wide'=96,'narrow'=8] {'wide'}, use_global_device_ids=true, to_apply=%region_7.13 | all-reduce | flops 4096 | bytes 32768 | tf_op jit(solution)/shard_map/psum | solution.py:56
  1230.7 5.8 cholesky.96
  1237.2 0.7 fusion.62
  1237.9 4.9 custom-call.12
  1242.8 1.7 fusion.43
  1244.5 1.0 gather_fusion.3
  1245.5 3.5 fusion.14
  1249.0 4.6 fusion
  1253.6 1.0 copy.69
  1254.7 298.7 %all-reduce.11.cloned.1.call-done = f32[64,3072]{1,0:T(8,128)} async-done(((f32[64,3072]{1,0:T(8,128)}), f32[64,3072]{1,0:T(8,128)}) %all-reduce.11.cloned.1.call-update) | async-done | bytes 786448 | tf_op jit(solution)/shard_map/psum | solution.py:64
  1553.4 2.2 fusion.38
  1555.6 27.7 %psum.63 = f32[64,64]{0,1:T(8,128)S(1)} all-reduce(f32[64,64]{0,1:T(8,128)S(1)} %fusion.38), channel_id=1, replica_groups=mesh['wide'=96,'narrow'=8] {'narrow'}, use_global_device_ids=true, to_apply=%region_9.15 | all-reduce | flops 4096 | bytes 32768 | tf_op jit(solution)/shard_map/psum | solution.py:67
  1583.4 5.8 cholesky.107
  1589.9 0.7 fusion.63
  1590.6 4.9 custom-call.13
  1595.5 2.9 fusion.36
  (45 shorter events, 3.6 us)
Async XLA Ops:
  7.2 99.5 %all-reduce.5.cloned.1.call-start = ((), (), s32[]{:S(2)}) async-start(), calls=%async_computation | async-start | bytes 1048576 | tf_op jit(solution)/shard_map/psum | solution.py:53
  12.1 5.1 copy-start.2
  17.3 5.7 copy-start.1
  22.9 742.6 %all-reduce.7.cloned.1.call-start = ((), (), s32[]{:S(2)}) async-start(), calls=%async_computation.1 | async-start | bytes 1572864 | tf_op jit(solution)/shard_map/psum | solution.py:64
  457.7 3.5 copy-start.3
  466.9 427.9 %all-reduce.9.cloned.1.call-start = ((), (), s32[]{:S(2)}) async-start(), calls=%async_computation.2 | async-start | bytes 1048576 | tf_op jit(solution)/shard_map/psum | solution.py:53
  821.4 732.0 %all-reduce.11.cloned.1.call-start = ((), (), s32[]{:S(2)}) async-start(), calls=%async_computation.3 | async-start | bytes 1572864 | tf_op jit(solution)/shard_map/psum | solution.py:64
  1244.5 4.5 copy-start
Sparse Core Ops, SparseCore 0:
  23.0 83.6 all-reduce.4
  467.0 298.5 all-reduce.6
  821.5 73.2 all-reduce.8
  1254.8 298.5 all-reduce.10
where the time goes:
time: 1610 us
  waiting for transfers between devices  754 us (47%)
  blocking collectives  724 us (45%)
  matrix products  51.9 us (3%)
  other arithmetic  51.7 us (3%)
    psum x2, blocking collectives, local(): user_gram = lax.psum(local_gram, 'wide') / all_users  668 us
    psum x2, waiting for transfers between devices, local(): item_sums = lax.psum(item_terms, 'wide')  597 us
    psum x2, waiting for transfers between devices, local(): user_sums = lax.psum(user_terms.reshape(vectors, user_rows), 'narrow')  157 us
    psum x2, blocking collectives, local(): item_gram = lax.psum(block_gram, 'narrow') / all_items  55.4 us
  transfers between devices with their start and end apart: 4, of which 4 were waited for; matrix products, arithmetic and copies ran while one was open for 0% of the time, Pallas kernels for 0%

commit v1 on v0

v1 whole, which is shorter than its diff:
```python
import jax
import jax.numpy as jnp
from jax import lax
from jax.experimental import pallas as pl
from jax.experimental.pallas import tpu as pltpu
from jax.sharding import PartitionSpec as P

ITERS = 2
GROUP = 16


def product_body(forward, blocks_out, vectors, src_ref, dst_ref, x_ref, tiles_ref, out_ref):
    step = pl.program_id(0)

    @pl.when(step == 0)
    def _():
        out_ref[...] = jnp.zeros_like(out_ref)

    terms = x_ref.shape[1] // vectors
    dims = (((1,), (1,)), ((), ())) if forward else (((1,), (0,)), ((), ()))
    for slot in range(GROUP):
        at = step * GROUP + slot
        product = lax.dot_general(
            x_ref[src_ref[at]], tiles_ref[slot], dims, preferred_element_type=jnp.float32
        )
        total = product[:vectors]
        for term in range(1, terms):
            total = total + product[term * vectors : (term + 1) * vectors]
        out_ref[dst_ref[at]] += total


def products(x, tiles, src, dst, blocks_out, vectors, forward):
    slots, tile, _ = tiles.shape
    blocks_in, rows, _ = x.shape

    def body(*refs):
        product_body(forward, blocks_out, vectors, *refs)

    out = pl.pallas_call(
        body,
        grid_spec=pltpu.PrefetchScalarGridSpec(
            num_scalar_prefetch=2,
            grid=(slots // GROUP,),
            in_specs=[
                pl.BlockSpec((blocks_in, rows, tile), lambda i, *_: (0, 0, 0)),
                pl.BlockSpec((GROUP, tile, tile), lambda i, *_: (i, 0, 0)),
            ],
            out_specs=pl.BlockSpec((blocks_out + 1, vectors, tile), lambda i, *_: (0, 0, 0)),
        ),
        out_shape=jax.ShapeDtypeStruct((blocks_out + 1, vectors, tile), jnp.float32),
        compiler_params=pltpu.CompilerParams(vmem_limit_bytes=32 * 1024 * 1024),
        name="products",
    )(src, dst, x, tiles)
    return out[:blocks_out]


def split_terms(x):
    high = x.astype(jnp.bfloat16)
    low = (x - high.astype(jnp.float32)).astype(jnp.bfloat16)
    return jnp.concatenate([high, low], axis=1)


def gram_of(raw):
    return jnp.einsum("bkc,bjc->kj", raw, raw, precision=lax.Precision.HIGHEST)


def inverse_factor(gram):
    factor = jnp.linalg.cholesky(gram)
    eye = jnp.eye(gram.shape[0], dtype=gram.dtype)
    return jax.scipy.linalg.solve_triangular(factor, eye, lower=True)


def apply_left(inverse, raw):
    return jnp.einsum("kj,bjc->bkc", inverse, raw, precision=lax.Precision.HIGHEST)


def sum_over(chunks, axis):
    got = lax.all_to_all(chunks, axis, 0, 0)
    mine = jnp.sum(got, axis=0, keepdims=True)
    copies = jnp.broadcast_to(mine, chunks.shape)
    return lax.all_to_all(copies, axis, 0, 0)


def local(tile_values, tile_row, tile_col, tile_count, user_degree, item_degree, start_vectors):
    vectors, item_rows = start_vectors.shape
    slot_count, tile, _ = tile_values.shape
    user_rows = user_degree.shape[0]
    user_blocks = user_rows // tile
    item_blocks = item_rows // tile
    wide_count = lax.axis_size("wide")
    narrow_count = lax.axis_size("narrow")
    all_users = user_rows * wide_count
    all_items = item_rows * narrow_count
    user_scale = lax.rsqrt(user_degree.astype(jnp.float32)).reshape(user_blocks, 1, tile)
    item_scale = lax.rsqrt(item_degree.astype(jnp.float32)).reshape(item_blocks, 1, tile)
    used = jnp.arange(slot_count, dtype=jnp.int32) < tile_count[0]
    row_out = jnp.where(used, tile_row, user_blocks)
    col_out = jnp.where(used, tile_col, item_blocks)

    def narrow_sum(terms, gram):
        data = terms.reshape(narrow_count, -1, tile)
        count = data.shape[1]
        if gram is None:
            return sum_over(data, "narrow").reshape(terms.shape), None
        wide_gram = jnp.pad(gram, ((0, 0), (0, tile - vectors))).reshape(narrow_count, -1, tile)
        both = sum_over(jnp.concatenate([data, wide_gram], axis=1), "narrow")
        return both[:, :count].reshape(terms.shape), both[:, count:].reshape(vectors, tile)[:, :vectors]

    def wide_sum(terms, gram):
        data = terms.reshape(wide_count, 1, -1)
        count = data.shape[2]
        wide_gram = jnp.pad(gram, ((0, wide_count - vectors), (0, tile - vectors))).reshape(wide_count, 1, tile)
        both = sum_over(jnp.concatenate([data, wide_gram], axis=2), "wide")
        return both[:, :, :count].reshape(terms.shape), both[:, 0, count:][:vectors, :vectors]

    start = jnp.transpose(start_vectors.reshape(vectors, item_blocks, tile), (1, 0, 2))
    item_source = (start * item_scale).astype(jnp.bfloat16)
    item_gram = None
    for step in range(ITERS):
        user_terms = products(item_source, tile_values, tile_col, row_out, user_blocks, vectors, True)
        user_sums, item_gram = narrow_sum(user_terms, item_gram)
        user_raw = user_sums * user_scale
        if item_gram is not None:
            user_raw = apply_left(inverse_factor(item_gram / all_items), user_raw)
        user_gram = gram_of(user_raw)
        user_source = split_terms(user_raw * user_scale)
        item_terms = products(user_source, tile_values, tile_row, col_out, item_blocks, vectors, False)
        item_sums, user_gram = wide_sum(item_terms, user_gram)
        user_inverse = inverse_factor(user_gram / all_users)
        item_raw = apply_left(user_inverse, item_sums) * item_scale
        item_gram = gram_of(item_raw)
        item_source = split_terms(item_raw * item_scale)
    copies = jnp.broadcast_to(item_gram[None], (narrow_count, vectors, vectors))
    item_gram = jnp.sum(lax.all_to_all(copies, "narrow", 0, 0), axis=0)
    item_inverse = inverse_factor(item_gram / all_items)
    user_vectors = jnp.einsum("kj,bjc->kbc", user_inverse, user_raw, precision=lax.Precision.HIGHEST)
    item_vectors = jnp.einsum("kj,bjc->kbc", item_inverse, item_raw, precision=lax.Precision.HIGHEST)
    return (user_vectors.reshape(vectors, user_rows), item_vectors.reshape(vectors, item_rows))


def solution(mesh):
    return jax.shard_map(
        local,
        mesh=mesh,
        in_specs=(
            P(("wide", "narrow"), None, None),
            P(("wide", "narrow")),
            P(("wide", "narrow")),
            P(("wide", "narrow")),
            P("wide"),
            P("narrow"),
            P(None, "narrow"),
        ),
        out_specs=(P(None, "wide"), P(None, "narrow")),
        check_vma=False,
    )
```

time: 1610 us -> 344 us (0.21)
  waiting for transfers between devices: 754 us -> 13.4 us
  blocking collectives: 724 us -> 222 us
  matrix products: 51.9 us -> 7.49 us
    psum x4 -> x0, waiting for transfers between devices: 754 us -> none  [the longest x2 597 us: local(): item_sums = lax.psum(item_terms, 'wide')]
    psum x4 -> x0, blocking collectives: 724 us -> none  [the longest x2 668 us: local(): user_gram = lax.psum(local_gram, 'wide') / all_users]
    all_to_all x0 -> x7, blocking collectives: none -> 222 us  [the longest x4 127 us: sum_over(): got = lax.all_to_all(chunks, axis, 0, 0)]
    dot_general x12 -> x9, matrix products: 43.7 us -> 6.48 us  [the longest x4 2.65 us: gram_of(): return jnp.einsum('bkc,bjc->kj', raw, raw, precision=lax.Precision.HIGHEST)]
  transfers between devices with their start and end apart: 4 -> 2, of which waited for: 4 -> 2; matrix products, arithmetic and copies ran while one was open for 0% -> 0% of each run, Pallas kernels for 0% -> 0%
where the time goes in v1:
time: 344 us; the launch traced here: 342 us
  blocking collectives  222 us (65%)
  other arithmetic  53.8 us (16%)
  local copies, waits for them, and re-layouts  15.6 us (5%)
  Pallas kernels  15.1 us (4%)
  waiting for transfers between devices  13.4 us (4%)
  starting transfers between devices  12.8 us (4%)
  matrix products  7.49 us (2%)
    all_to_all x4, blocking collectives, sum_over(): got = lax.all_to_all(chunks, axis, 0, 0)  127 us
    all_to_all x3, blocking collectives, sum_over(): return lax.all_to_all(copies, axis, 0, 0)  95.1 us
    another operation x12, other arithmetic, inverse_factor(): factor = jnp.linalg.cholesky(gram)  26.1 us
    another operation x8, other arithmetic, inverse_factor(): return jax.scipy.linalg.solve_triangular(factor, eye, lower=True)  22.2 us
    pallas_call x4, Pallas kernels, products(): pl.pallas_call(body, grid_spec=pltpu.PrefetchScalarGridSpec(num_scalar_pr...  15.1 us
    unnamed x25, local copies, waits for them, and re-layouts  10.3 us
    all_to_all x1, waiting for transfers between devices, sum_over(): return lax.all_to_all(copies, axis, 0, 0)  9.47 us
    all_to_all x1, starting transfers between devices, local(): item_gram = jnp.sum(lax.all_to_all(copies, 'narrow', 0, 0), axis=0)  8.21 us
  transfers between devices with their start and end apart: 2, of which 2 were waited for; matrix products, arithmetic and copies ran while one was open for 0% of the time, Pallas kernels for 0%

profile of v1, /device:TPU:1, one launch (start us, length us, event | category | flops | bytes accessed | tf_op | source)
XLA Modules:
  0.0 342.2 jit_solution(11440764639748071330)
XLA Ops:
  0.6 0.8 rsqrt_bitcast_fusion
  2.2 0.7 compare_select_fusion.refs_1_
  2.9 2.2 copy-done.1
  5.0 0.7 copy-done.6
  5.7 4.4 %products.4 = f32[17,64,128]{2,1,0:T(8,128)S(1)} custom-call(s32[128]{0:T(128)S(1)} %copy-done.6, s32[128]{0:T(128)S(1)} %compare_select_fusion.refs_1_, bf16[24,64,128]{2,1,0:T(8,128)(2,1)S(1)} %fusion.5.refs_2_, bf16[128,128,128]{2,1,0:T(8,128)(2,1)S(1)} %copy-done.1), custom_call_target="tpu_custom_call" | custom-call | tf_op jit(solution)/shard_map/products/pallas_call | solution.py:39
  10.1 22.3 %all_to_all.45 = f32[8,128,128]{2,1,0:T(8,128)S(1)} all-to-all(f32[8,128,128]{2,1,0:T(8,128)S(1)} %bitcast.137), channel_id=1, replica_groups=mesh['wide'=96,'narrow'=8] {'narrow'}, dimensions={0} | all-to-all | bytes 1048576 | tf_op jit(solution)/shard_map/all_to_all | solution.py:78
  32.5 0.8 broadcast_in_dim.20
  33.3 4.6 %all-to-all-start.1 = ((f32[8,128,128]{2,1,0:T(8,128)}), f32[8,128,128]{2,1,0:T(8,128)S(1)}, u32[]{:S(2)}, u32[]{:S(2)}) async-start(f32[8,128,128]{2,1,0:T(8,128)} %broadcast_in_dim.20), calls=%async_computation.1 | async-start | bytes 1048576 | tf_op jit(solution)/shard_map/all_to_all | solution.py:81
  37.9 9.5 %all-to-all-done.1 = f32[8,128,128]{2,1,0:T(8,128)S(1)} async-done(((f32[8,128,128]{2,1,0:T(8,128)}), f32[8,128,128]{2,1,0:T(8,128)S(1)}, u32[]{:S(2)}, u32[]{:S(2)}) %all-to-all-start.1) | async-done | bytes 524320 | tf_op jit(solution)/shard_map/all_to_all | solution.py:81
  47.6 2.2 copy-done.2
  49.7 3.1 products.5
  53.0 0.8 copy-done.5
  54.9 0.7 pad_maximum_fusion
  55.6 46.7 %all_to_all.46 = f32[96,1,2176]{2,1,0:T(1,128)S(1)} all-to-all(f32[96,1,2176]{2,1,0:T(1,128)S(1)} %pad_maximum_fusion), channel_id=1, replica_groups=mesh['wide'=96,'narrow'=8] {'wide'}, dimensions={0} | all-to-all | bytes 1671168 | tf_op jit(solution)/shard_map/all_to_all | solution.py:78
  103.2 41.1 %all_to_all.47 = f32[96,1,2176]{2,1,0:T(1,128)S(1)} all-to-all(f32[96,1,2176]{2,1,0:T(1,128)S(1)} %broadcast_in_dim.21), channel_id=1, replica_groups=mesh['wide'=96,'narrow'=8] {'wide'}, dimensions={0} | all-to-all | bytes 1671168 | tf_op jit(solution)/shard_map/all_to_all | solution.py:81
  144.6 5.8 %cholesky.74 = f32[64,64]{1,0:T(8,128)S(1)} custom-call(f32[64,64]{1,0:T(8,128)S(1)} %fusion.22), custom_call_target="Cholesky" | custom-call | tf_op jit(solution)/shard_map/jit(cholesky)/cholesky | solution.py:68
  151.1 0.7 fusion.11
  151.8 4.9 %custom-call.8 = f32[1,64,64]{1,2,0:T(8,128)S(1)} custom-call(f32[1,64,64]{2,1,0:T(8,128)S(1)} %fusion.11), custom_call_target="InvertDiagBlocksLowerTriangular" | custom-call | tf_op jit(solution)/shard_map/jit(_solve_triangular)/triangular_solve | solution.py:70
  157.0 0.9 multiply_convert_fusion
  158.1 1.1 copy-done.3
  159.2 4.5 %products.6 = f32[17,64,128]{2,1,0:T(8,128)S(1)} custom-call(s32[128]{0:T(128)S(1)} %copy-done.7, s32[128]{0:T(128)S(1)} %compare_select_fusion.refs_1_, bf16[24,128,128]{2,1,0:T(8,128)(2,1)S(1)} %pad_maximum_fusion.2.refs_2_, bf16[128,128,128]{2,1,0:T(8,128)(2,1)S(1)} %copy-done.3), custom_call_target="tpu_custom_call" | custom-call | tf_op jit(solution)/shard_map/products/pallas_call | solution.py:39
  163.7 0.8 convolution_bitcast_fusion.4
  164.6 17.7 %all_to_all.48 = f32[8,136,128]{2,1,0:T(8,128)S(1)} all-to-all(f32[8,136,128]{2,1,0:T(8,128)S(1)} %pad_maximum_fusion.3), channel_id=1, replica_groups=mesh['wide'=96,'narrow'=8] {'narrow'}, dimensions={0} | all-to-all | bytes 1114112 | tf_op jit(solution)/shard_map/all_to_all | solution.py:78
  182.3 13.1 %all_to_all.49 = f32[8,136,128]{2,1,0:T(8,128)S(1)} all-to-all(f32[8,136,128]{2,1,0:T(8,128)S(1)} %broadcast_in_dim.22), channel_id=1, replica_groups=mesh['wide'=96,'narrow'=8] {'narrow'}, dimensions={0} | all-to-all | bytes 1114112 | tf_op jit(solution)/shard_map/all_to_all | solution.py:81
  195.7 5.8 %cholesky.85 = f32[64,64]{1,0:T(8,128)S(1)} custom-call(f32[64,64]{1,0:T(8,128)S(1)} %fusion.20), custom_call_target="Cholesky" | custom-call | tf_op jit(solution)/shard_map/jit(cholesky)/cholesky | solution.py:68
  202.2 0.7 fusion.12
  202.9 4.9 %custom-call.9 = f32[1,64,64]{1,2,0:T(8,128)S(1)} custom-call(f32[1,64,64]{2,1,0:T(8,128)S(1)} %fusion.12), custom_call_target="InvertDiagBlocksLowerTriangular" | custom-call | tf_op jit(solution)/shard_map/jit(_solve_triangular)/triangular_solve | solution.py:70
  208.1 0.7 multiply_convert_fusion.1
  208.8 2.2 copy-done.4
  211.0 3.1 products.7
  214.8 0.7 pad_maximum_fusion.1
  215.5 40.5 %all_to_all.50 = f32[96,1,2176]{2,1,0:T(1,128)S(1)} all-to-all(f32[96,1,2176]{2,1,0:T(1,128)S(1)} %pad_maximum_fusion.1), channel_id=1, replica_groups=mesh['wide'=96,'narrow'=8] {'wide'}, dimensions={0} | all-to-all | bytes 1671168 | tf_op jit(solution)/shard_map/all_to_all | solution.py:78
  256.9 40.8 %all_to_all.51 = f32[96,1,2176]{2,1,0:T(1,128)S(1)} all-to-all(f32[96,1,2176]{2,1,0:T(1,128)S(1)} %broadcast_in_dim.23), channel_id=1, replica_groups=mesh['wide'=96,'narrow'=8] {'wide'}, dimensions={0} | all-to-all | bytes 1671168 | tf_op jit(solution)/shard_map/all_to_all | solution.py:81
  298.0 5.8 %cholesky.96 = f32[64,64]{1,0:T(8,128)S(1)} custom-call(f32[64,64]{1,0:T(8,128)S(1)} %fusion.18), custom_call_target="Cholesky" | custom-call | tf_op jit(solution)/shard_map/jit(cholesky)/cholesky | solution.py:68
  304.5 0.7 fusion.13
  305.2 4.9 %custom-call.10 = f32[1,64,64]{1,2,0:T(8,128)S(1)} custom-call(f32[1,64,64]{2,1,0:T(8,128)S(1)} %fusion.13), custom_call_target="InvertDiagBlocksLowerTriangular" | custom-call | tf_op jit(solution)/shard_map/jit(_solve_triangular)/triangular_solve | solution.py:70
  310.4 0.8 fusion
  311.2 0.8 convolution_bitcast_fusion.3
  312.0 0.8 reshape.101
  312.9 8.2 %all-to-all-start.8 = ((f32[8,1,4096]{2,1,0:T(1,128)}), f32[8,1,4096]{2,1,0:T(1,128)S(1)}, u32[]{:S(2)}, u32[]{:S(2)}) async-start(f32[8,1,4096]{2,1,0:T(1,128)} %reshape.101), calls=%async_computation.8 | async-start | bytes 262144 | tf_op jit(solution)/shard_map/all_to_all | solution.py:134
  321.6 0.8 copy.65
  322.5 3.9 %all-to-all-done.8 = f32[8,1,4096]{2,1,0:T(1,128)S(1)} async-done(((f32[8,1,4096]{2,1,0:T(1,128)}), f32[8,1,4096]{2,1,0:T(1,128)S(1)}, u32[]{:S(2)}, u32[]{:S(2)}) %all-to-all-start.8) | async-done | bytes 131104 | tf_op jit(solution)/shard_map/all_to_all | solution.py:134
  326.9 1.0 reduce.6
  328.2 5.8 %cholesky.107 = f32[64,64]{1,0:T(8,128)S(1)} custom-call(f32[64,64]{1,0:T(8,128)S(1)} %fusion.16), custom_call_target="Cholesky" | custom-call | tf_op jit(solution)/shard_map/jit(cholesky)/cholesky | solution.py:68
  334.7 0.7 fusion.14
  335.4 4.9 %custom-call.11 = f32[1,64,64]{1,2,0:T(8,128)S(1)} custom-call(f32[1,64,64]{2,1,0:T(8,128)S(1)} %fusion.14), custom_call_target="InvertDiagBlocksLowerTriangular" | custom-call | tf_op jit(solution)/shard_map/jit(_solve_triangular)/triangular_solve | solution.py:70
  340.5 0.8 convolution_bitcast_fusion
  341.3 0.9 copy.64
  (80 shorter events, 10.2 us)
Async XLA Ops:
  0.6 1.5 copy-start
  2.9 2.2 copy-start.1
  5.0 0.7 copy-start.6
  10.1 27.7 %copy-start.7 = (s32[128]{0:T(128)S(1)}, s32[128]{0:T(128)}, u32[]{:S(2)}) copy-start(s32[128]{0:T(128)} %refs_0_.6) | copy-start | bytes 1540
  10.1 27.7 %copy-start.9 = (s32[2048]{0:T(1024)S(1)}, s32[2048]{0:T(1024)}, u32[]{:S(2)}) copy-start(s32[2048]{0:T(1024)} %param.14) | copy-start | bytes 24580
  33.3 14.3 %copy-start.8 = (s32[128]{0:T(128)S(1)}, s32[128]{0:T(128)}, u32[]{:S(2)}) copy-start(s32[128]{0:T(128)} %refs_0_.7) | copy-start | bytes 1540
  33.3 14.1 %all-to-all-start.1 = ((f32[8,128,128]{2,1,0:T(8,128)}), f32[8,128,128]{2,1,0:T(8,128)S(1)}, u32[]{:S(2)}, u32[]{:S(2)}) async-start(f32[8,128,128]{2,1,0:T(8,128)} %broadcast_in_dim.20), calls=%async_computation.1 | async-start | bytes 1048576 | tf_op jit(solution)/shard_map/all_to_all | solution.py:81
  47.6 2.2 copy-start.2
  52.9 0.9 copy-start.5
  53.8 1.1 slice-start
  157.0 2.2 copy-start.3
  208.8 2.2 copy-start.4
  312.9 13.5 %all-to-all-start.8 = ((f32[8,1,4096]{2,1,0:T(1,128)}), f32[8,1,4096]{2,1,0:T(1,128)S(1)}, u32[]{:S(2)}, u32[]{:S(2)}) async-start(f32[8,1,4096]{2,1,0:T(1,128)} %reshape.101), calls=%async_computation.8 | async-start | bytes 262144 | tf_op jit(solution)/shard_map/all_to_all | solution.py:134

commit v2 on v0

v2 whole, which is shorter than its diff:
```python
import jax
import jax.numpy as jnp
from jax import lax
from jax.experimental import pallas as pl
from jax.experimental.pallas import tpu as pltpu
from jax.sharding import Mesh, PartitionSpec as P

ITERS = 2
GROUP = 16
Y_CHIPS = 8
SUB = 8
FULL = lax.Precision.HIGHEST
VMEM = pl.BlockSpec(memory_space=pltpu.VMEM)


def dot(a, b, last=False):
    dims = (((1,), (1,)), ((), ())) if last else (((1,), (0,)), ((), ()))
    return lax.dot_general(a, b, dims, precision=FULL, preferred_element_type=jnp.float32)


def inverse_factor(panels):
    vectors = len(panels) * SUB
    lane = lax.broadcasted_iota(jnp.int32, (SUB, 2 * vectors), 1)
    sub = lax.broadcasted_iota(jnp.int32, (SUB, 2 * vectors), 0)
    rows = []
    for p, panel in enumerate(panels):
        unit = jnp.where(lane == vectors + p * SUB + sub, 1.0, 0.0)
        rows.append(jnp.where(lane < vectors, panel, unit))

    def spread(panel, p):
        return [jnp.broadcast_to(panel[:, p * SUB + q : p * SUB + q + 1], panel.shape) for q in range(SUB)]

    def row(value, q):
        return jnp.broadcast_to(value[q : q + 1, :], value.shape)

    for p in range(len(panels)):
        cols = spread(rows[p], p)
        pivots, heads, inverses = [], [], []
        scale = jnp.ones_like(rows[p])
        for q in range(SUB):
            head = row(rows[p], q)
            tops = [None if t < q else row(cols[t], q) for t in range(SUB)]
            inverse = 1.0 / tops[q]
            pivots.append(head)
            heads.append(tops)
            inverses.append(inverse)
            scale = jnp.where(sub == q, tops[q], scale)
            factor = jnp.where(sub > q, cols[q] * inverse, 0.0)
            rows[p] = rows[p] - factor * head
            for t in range(q + 1, SUB):
                cols[t] = cols[t] - factor * tops[t]
        for r in range(p + 1, len(panels)):
            cols = spread(rows[r], p)
            for q in range(SUB):
                factor = cols[q] * inverses[q]
                rows[r] = rows[r] - factor * pivots[q]
                for t in range(q + 1, SUB):
                    cols[t] = cols[t] - factor * heads[q][t]
        rows[p] = rows[p] * lax.rsqrt(scale)
    return jnp.concatenate(rows, axis=0)[:, vectors:]


def padded(gram):
    return jnp.concatenate([gram, jnp.zeros_like(gram)], axis=1)


def phase(data, scale, tiles, src, dst, blocks_out, forward, gram_count, round_first, send_gram, keep_raw):
    slots, tile, _ = tiles.shape
    blocks, _, _ = scale.shape
    chunks = data.shape[0]
    vectors = tile // 2
    per_chunk = blocks // chunks
    have_gram = gram_count is not None
    terms = 1 if round_first else 2
    out_chunks = Y_CHIPS
    out_per = blocks_out // out_chunks
    out_rows = out_per * vectors + (SUB if send_gram else 0)
    steps = slots // GROUP
    dims = (((1,), (1,)), ((), ())) if forward else (((1,), (0,)), ((), ()))

    def body(src_ref, dst_ref, data_ref, scale_ref, tiles_ref, out_ref, *rest):
        if keep_raw:
            raw_ref, x_ref, sums_ref, gram_ref = rest
        else:
            x_ref, sums_ref, gram_ref = rest
        step = pl.program_id(0)

        @pl.when(step == 0)
        def _():
            sums_ref[...] = jnp.zeros_like(sums_ref)
            inverse = None
            if have_gram:
                at = per_chunk * vectors
                inverse = inverse_factor([data_ref[c, at : at + SUB, :] * (1.0 / gram_count) for c in range(chunks)])
            gram = jnp.zeros((vectors, vectors), jnp.float32)
            for block in range(blocks):
                at = (block % per_chunk) * vectors
                raw = data_ref[block // per_chunk, at : at + vectors, :]
                weight = scale_ref[block]
                if not round_first:
                    if have_gram:
                        raw = dot(inverse, raw)
                    raw = raw * weight
                if keep_raw:
                    raw_ref[block] = raw
                if send_gram:
                    gram = gram + dot(raw, raw, last=True)
                source = raw * weight
                high = source.astype(jnp.bfloat16)
                x_ref[block, :vectors, :] = high
                if terms == 2:
                    x_ref[block, vectors:, :] = (source - high.astype(jnp.float32)).astype(jnp.bfloat16)
            if send_gram:
                gram_ref[...] = padded(gram)

        for slot in range(GROUP):
            at = step * GROUP + slot
            product = lax.dot_general(
                x_ref[src_ref[at]], tiles_ref[slot], dims, preferred_element_type=jnp.float32
            )
            if terms == 2:
                product = product[:vectors] + product[vectors:]
            sums_ref[dst_ref[at]] += product

        @pl.when(step == steps - 1)
        def _():
            for block in range(blocks_out):
                at = (block % out_per) * vectors
                out_ref[block // out_per, at : at + vectors, :] = sums_ref[block]
            if send_gram:
                for c in range(out_chunks):
                    out_ref[c, out_per * vectors :, :] = gram_ref[c * SUB : (c + 1) * SUB, :]

    out_shape = [jax.ShapeDtypeStruct((out_chunks, out_rows, tile), jnp.float32)]
    out_specs = [pl.BlockSpec((out_chunks, out_rows, tile), lambda i, *_: (0, 0, 0))]
    if keep_raw:
        out_shape.append(jax.ShapeDtypeStruct((blocks, vectors, tile), jnp.float32))
        out_specs.append(pl.BlockSpec((blocks, vectors, tile), lambda i, *_: (0, 0, 0)))
    return pl.pallas_call(
        body,
        grid_spec=pltpu.PrefetchScalarGridSpec(
            num_scalar_prefetch=2,
            grid=(steps,),
            in_specs=[
                pl.BlockSpec(data.shape, lambda i, *_: (0, 0, 0)),
                pl.BlockSpec(scale.shape, lambda i, *_: (0, 0, 0)),
                pl.BlockSpec((GROUP, tile, tile), lambda i, *_: (i, 0, 0)),
            ],
            out_specs=out_specs,
            scratch_shapes=[
                pltpu.VMEM((blocks, terms * vectors, tile), jnp.bfloat16),
                pltpu.VMEM((blocks_out + 1, vectors, tile), jnp.float32),
                pltpu.VMEM((vectors, tile), jnp.float32),
            ],
        ),
        out_shape=out_shape,
        compiler_params=pltpu.CompilerParams(vmem_limit_bytes=VMEM_LIMIT),
        name="forward" if forward else "backward",
    )(src, dst, data, scale, tiles)


VMEM_LIMIT = 32 * 1024 * 1024


def call(body, inputs, shapes, name):
    return pl.pallas_call(
        body,
        in_specs=[VMEM] * len(inputs),
        out_specs=[VMEM] * len(shapes),
        out_shape=[jax.ShapeDtypeStruct(s, jnp.float32) for s in shapes],
        compiler_params=pltpu.CompilerParams(vmem_limit_bytes=VMEM_LIMIT),
        name=name,
    )(*inputs)


def total(ref, begin, end):
    value = ref[0, begin:end, :]
    for c in range(1, ref.shape[0]):
        value = value + ref[c, begin:end, :]
    return value


def exchange(data, axis):
    return lax.all_to_all(data, axis, 0, 0)


def narrow_sum(chunks):
    def body(got_ref, out_ref):
        mine = total(got_ref, 0, got_ref.shape[1])
        for c in range(out_ref.shape[0]):
            out_ref[c] = mine

    (copies,) = call(body, [exchange(chunks, "narrow")], [chunks.shape], "sum_copies")
    return exchange(copies, "narrow")


def wide_sum(chunks, z_count):
    rows, tile = chunks.shape[1] - SUB, chunks.shape[2]
    part = rows // z_count

    def split(got_ref, out_ref):
        last = total(got_ref, rows, rows + SUB)
        for c in range(z_count):
            out_ref[c, :part, :] = total(got_ref, c * part, (c + 1) * part)
            out_ref[c, part:, :] = last

    def spread(got_ref, out_ref, last_ref):
        mine = total(got_ref, 0, part)
        for c in range(z_count):
            out_ref[c] = mine
        last_ref[...] = total(got_ref, part, part + SUB)

    def copies(got_ref, last_ref, out_ref):
        for c in range(out_ref.shape[0]):
            for z in range(z_count):
                out_ref[c, z * part : (z + 1) * part, :] = got_ref[z]
            out_ref[c, rows:, :] = last_ref[...]

    (parts,) = call(split, [exchange(chunks, "y")], [(z_count, part + SUB, tile)], "sum_split")
    mine, last = call(spread, [exchange(parts, "z")], [(z_count, part, tile), (SUB, tile)], "sum_spread")
    (back,) = call(copies, [exchange(mine, "z"), last], [chunks.shape], "copies")
    return exchange(back, "y")


def finish_items(data, scale, user_count):
    chunks, rows, tile = data.shape
    blocks = scale.shape[0]
    vectors = tile // 2
    per_chunk = blocks // chunks

    def body(data_ref, scale_ref, raw_ref, gram_ref, inverse_ref):
        at = per_chunk * vectors
        inverse = inverse_factor([data_ref[c, at : at + SUB, :] * (1.0 / user_count) for c in range(chunks)])
        inverse_ref[...] = inverse
        gram = jnp.zeros((vectors, vectors), jnp.float32)
        for block in range(blocks):
            at = (block % per_chunk) * vectors
            raw = dot(inverse, data_ref[block // per_chunk, at : at + vectors, :]) * scale_ref[block]
            raw_ref[block] = raw
            gram = gram + dot(raw, raw, last=True)
        packed = jnp.concatenate([gram[: vectors // 2], gram[vectors // 2 :]], axis=1)
        for c in range(gram_ref.shape[0]):
            gram_ref[c] = packed

    shapes = [(blocks, vectors, tile), (Y_CHIPS, vectors // 2, tile), (vectors, vectors)]
    return call(body, [data, scale], shapes, "finish_items")


def finish_users(raw, inverse):
    blocks, vectors, tile = raw.shape

    def body(raw_ref, inverse_ref, out_ref):
        for block in range(blocks):
            out_ref[:, block * tile : (block + 1) * tile] = dot(inverse_ref[...], raw_ref[block])

    return call(body, [raw, inverse], [(vectors, blocks * tile)], "finish_users")[0]


def finish_vectors(raw, grams, item_count):
    blocks, vectors, tile = raw.shape

    def body(raw_ref, grams_ref, out_ref):
        gram = total(grams_ref, 0, vectors // 2) * (1.0 / item_count)
        gram = jnp.concatenate([gram[:, :vectors], gram[:, vectors:]], axis=0)
        gram = padded(gram)
        inverse = inverse_factor([gram[at : at + SUB] for at in range(0, vectors, SUB)])
        for block in range(blocks):
            out_ref[:, block * tile : (block + 1) * tile] = dot(inverse, raw_ref[block])

    return call(body, [raw, grams], [(vectors, blocks * tile)], "finish_vectors")[0]


def local(tile_values, tile_row, tile_col, tile_count, user_degree, item_degree, start_vectors):
    vectors, item_rows = start_vectors.shape
    slot_count, tile, _ = tile_values.shape
    user_rows = user_degree.shape[0]
    user_blocks = user_rows // tile
    item_blocks = item_rows // tile
    z_count = lax.axis_size("z")
    all_users = user_rows * lax.axis_size("y") * z_count
    all_items = item_rows * lax.axis_size("narrow")
    user_scale = lax.rsqrt(user_degree.astype(jnp.float32)).reshape(user_blocks, 1, tile)
    item_scale = lax.rsqrt(item_degree.astype(jnp.float32)).reshape(item_blocks, 1, tile)
    used = jnp.arange(slot_count, dtype=jnp.int32) < tile_count[0]
    row_out = jnp.where(used, tile_row, user_blocks)
    col_out = jnp.where(used, tile_col, item_blocks)

    item_data = jnp.transpose(start_vectors.reshape(vectors, item_blocks, tile), (1, 0, 2))
    for step in range(ITERS):
        first, last = step == 0, step == ITERS - 1
        (terms,) = phase(
            item_data, item_scale, tile_values, tile_col, row_out, user_blocks, True,
            None if first else all_users, first, not first, False,
        )
        user_data = narrow_sum(terms)
        out = phase(
            user_data, user_scale, tile_values, tile_row, col_out, item_blocks, False,
            None if first else all_items, False, True, last,
        )
        item_data = wide_sum(out[0], z_count)
    user_raw = out[1]
    item_raw, grams, user_inverse = finish_items(item_data, item_scale, all_users)
    grams = exchange(grams, "narrow")
    user_vectors = finish_users(user_raw, user_inverse)
    item_vectors = finish_vectors(item_raw, grams, all_items)
    return (user_vectors, item_vectors)


def solution(mesh):
    wide_count, narrow_count = mesh.devices.shape
    grid = mesh.devices.reshape(Y_CHIPS, wide_count // Y_CHIPS, narrow_count)
    owner = ("y", "z", "narrow")
    return jax.shard_map(
        local,
        mesh=Mesh(grid, owner),
        in_specs=(
            P(owner, None, None),
            P(owner),
            P(owner),
            P(owner),
            P(("y", "z")),
            P("narrow"),
            P(None, "narrow"),
        ),
        out_specs=(P(None, ("y", "z")), P(None, "narrow")),
        check_vma=False,
    )
```

time: 1610 us -> 284 us (0.18)
  waiting for transfers between devices: 754 us -> 13.4 us
  blocking collectives: 724 us -> 210 us
  matrix products: 51.9 us -> 0 us
  other arithmetic: 51.7 us -> 1.39 us
  Pallas kernels: 0 us -> 38.2 us
    psum x4 -> x0, waiting for transfers between devices: 754 us -> none  [the longest x2 597 us: local(): item_sums = lax.psum(item_terms, 'wide')]
    psum x4 -> x0, blocking collectives: 724 us -> none  [the longest x2 668 us: local(): user_gram = lax.psum(local_gram, 'wide') / all_users]
    all_to_all x0 -> x11, blocking collectives: none -> 210 us  [exchange(): return lax.all_to_all(data, axis, 0, 0)]
    another operation x20 -> x0, other arithmetic: 48.3 us -> none  [the longest x6 13 us: local(): factor_two = jnp.linalg.cholesky(item_gram)]
    dot_general x12 -> x0, matrix products: 43.7 us -> none  [the longest x4 18.5 us: block_terms(): jnp.einsum('tb,ktr->kbr', target_onehot, products, precision=lax.Precisio...]
    pallas_call x0 -> x15, Pallas kernels: none -> 38.2 us  [the longest x4 26 us: phase(): pl.pallas_call(body, grid_spec=pltpu.PrefetchScalarGridSpec(num_scalar_pr...]
  transfers between devices with their start and end apart: 4 -> 2, of which waited for: 4 -> 2; matrix products, arithmetic and copies ran while one was open for 0% -> 0% of each run, Pallas kernels for 0% -> 0%
where the time goes in v2:
time: 284 us; the launch traced here: 283 us
  blocking collectives  210 us (74%)
  Pallas kernels  38.2 us (13%)
  starting transfers between devices  13.6 us (5%)
  waiting for transfers between devices  13.4 us (5%)
  local copies, waits for them, and re-layouts  5.14 us (2%)
    all_to_all x11, blocking collectives, exchange(): return lax.all_to_all(data, axis, 0, 0)  210 us
    pallas_call x4, Pallas kernels, phase(): pl.pallas_call(body, grid_spec=pltpu.PrefetchScalarGridSpec(num_scalar_pr...  26 us
    all_to_all x2, starting transfers between devices, exchange(): return lax.all_to_all(data, axis, 0, 0)  13.6 us
    all_to_all x2, waiting for transfers between devices, exchange(): return lax.all_to_all(data, axis, 0, 0)  13.4 us
    pallas_call x11, Pallas kernels, call(): pl.pallas_call(body, in_specs=[VMEM] * len(inputs), out_specs=[VMEM] * le...  12.2 us
  transfers between devices with their start and end apart: 2, of which 2 were waited for; matrix products, arithmetic and copies ran while one was open for 0% of the time, Pallas kernels for 0%

profile of v2, /device:TPU:1, one launch (start us, length us, event | category | flops | bytes accessed | tf_op | source)
XLA Modules:
  0.0 283.1 jit_solution(13811292012430684199)
XLA Ops:
  0.6 0.0 copy-start
  1.4 0.7 convert_rsqrt_fusion
  2.1 0.0 copy-done
  2.1 0.1 bitcast_bitcast_fusion.data_ref
  2.2 0.7 compare_select_fusion.dst_ref
  2.8 0.0 copy-start.1
  2.8 2.2 copy-done.1
  5.0 0.0 copy-start.5
  5.0 0.7 copy-done.5
  5.7 0.0 copy-start.6
  5.7 0.0 copy-start.7
  5.7 0.0 copy-start.4
  5.7 4.5 %forward.2 = f32[8,128,128]{2,1,0:T(8,128)S(1)} custom-call(s32[128]{0:T(128)S(1)} %copy-done.5, s32[128]{0:T(128)S(1)} %compare_select_fusion.dst_ref, f32[24,64,128]{2,1,0:T(8,128)S(1)} %bitcast_bitcast_fusion.data_ref, f32[24,1,128]{2,1,0:T(1,128)S(1)} %bitcast.12, bf16[128,128,128]{2,1,0:T(8,128)(2,1)S(1)} %copy-done.1), custom_call_target="tpu_custom_call" | custom-call | tf_op jit(solution)/shard_map/forward/pallas_call | solution.py:139
  10.2 22.3 %all_to_all.65.got_ref = f32[8,128,128]{2,1,0:T(8,128)S(1)} all-to-all(f32[8,128,128]{2,1,0:T(8,128)S(1)} %forward.2), channel_id=1, replica_groups=mesh['y'=8,'z'=12,'narrow'=8] {'narrow'}, dimensions={0} | all-to-all | bytes 1048576 | tf_op jit(solution)/shard_map/all_to_all | solution.py:184
  32.4 0.8 sum_copies.2
  33.3 4.4 %all-to-all-start.1 = ((f32[8,128,128]{2,1,0:T(8,128)}), f32[8,128,128]{2,1,0:T(8,128)S(1)}, u32[]{:S(2)}, u32[]{:S(2)}) async-start(f32[8,128,128]{2,1,0:T(8,128)} %sum_copies.2), calls=%async_computation.1 | async-start | bytes 1048576 | tf_op jit(solution)/shard_map/all_to_all | solution.py:184
  37.7 0.0 copy-done.6
  37.7 0.0 copy-done.7
  37.8 9.5 %all-to-all-done.1.data_ref = f32[8,128,128]{2,1,0:T(8,128)S(1)} async-done(((f32[8,128,128]{2,1,0:T(8,128)}), f32[8,128,128]{2,1,0:T(8,128)S(1)}, u32[]{:S(2)}, u32[]{:S(2)}) %all-to-all-start.1) | async-done | bytes 524320 | tf_op jit(solution)/shard_map/all_to_all | solution.py:184
  47.2 0.0 copy-done.4
  47.2 0.0 copy-start.2
  47.2 2.2 copy-done.2
  49.4 4.1 %backward.2 = f32[8,200,128]{2,1,0:T(8,128)S(1)} custom-call(s32[128]{0:T(128)S(1)} %copy-done.4, s32[128]{0:T(128)S(1)} %compare_select_fusion.1.dst_ref, f32[8,128,128]{2,1,0:T(8,128)S(1)} %all-to-all-done.1.data_ref, f32[16,1,128]{2,1,0:T(1,128)S(1)} %bitcast.15, bf16[128,128,128]{2,1,0:T(8,128)(2,1)S(1)} %copy-done.2), custom_call_target="tpu_custom_call" | custom-call | tf_op jit(solution)/shard_map/backward/pallas_call | solution.py:139
  53.5 0.0 copy-start.3
  53.5 25.0 %all_to_all.66.got_ref = f32[8,200,128]{2,1,0:T(8,128)S(1)} all-to-all(f32[8,200,128]{2,1,0:T(8,128)S(1)} %backward.2), channel_id=1, replica_groups=mesh['y'=8,'z'=12,'narrow'=8] {'y'}, dimensions={0} | all-to-all | bytes 1638400 | tf_op jit(solution)/shard_map/all_to_all | solution.py:184
  78.5 21.8 %all_to_all.67.got_ref = f32[12,24,128]{2,1,0:T(8,128)S(1)} all-to-all(f32[12,24,128]{2,1,0:T(8,128)S(1)} %sum_split.2), channel_id=1, replica_groups=mesh['y'=8,'z'=12,'narrow'=8] {'z'}, dimensions={0} | all-to-all | bytes 294912 | tf_op jit(solution)/shard_map/all_to_all | solution.py:184
  100.4 12.8 %all_to_all.68.got_ref = f32[12,16,128]{2,1,0:T(8,128)S(1)} all-to-all(f32[12,16,128]{2,1,0:T(8,128)S(1)} %get-tuple-element.11), channel_id=1, replica_groups=mesh['y'=8,'z'=12,'narrow'=8] {'z'}, dimensions={0} | all-to-all | bytes 196608 | tf_op jit(solution)/shard_map/all_to_all | solution.py:184
  113.2 0.1 copies.2
  113.2 23.0 %all_to_all.69.data_ref = f32[8,200,128]{2,1,0:T(8,128)S(1)} all-to-all(f32[8,200,128]{2,1,0:T(8,128)S(1)} %copies.2), channel_id=1, replica_groups=mesh['y'=8,'z'=12,'narrow'=8] {'y'}, dimensions={0} | all-to-all | bytes 1638400 | tf_op jit(solution)/shard_map/all_to_all | solution.py:184
  136.2 0.0 copy-done.3
  136.2 10.0 %forward.3 = f32[8,136,128]{2,1,0:T(8,128)S(1)} custom-call(s32[128]{0:T(128)S(1)} %copy-done.6, s32[128]{0:T(128)S(1)} %compare_select_fusion.dst_ref, f32[8,200,128]{2,1,0:T(8,128)S(1)} %all_to_all.69.data_ref, f32[24,1,128]{2,1,0:T(1,128)S(1)} %bitcast.13, bf16[128,128,128]{2,1,0:T(8,128)(2,1)S(1)} %copy-done.3), custom_call_target="tpu_custom_call" | custom-call | tf_op jit(solution)/shard_map/forward/pallas_call | solution.py:139
  146.3 18.4 %all_to_all.70.got_ref = f32[8,136,128]{2,1,0:T(8,128)S(1)} all-to-all(f32[8,136,128]{2,1,0:T(8,128)S(1)} %forward.3), channel_id=1, replica_groups=mesh['y'=8,'z'=12,'narrow'=8] {'narrow'}, dimensions={0} | all-to-all | bytes 1114112 | tf_op jit(solution)/shard_map/all_to_all | solution.py:184
  164.7 13.1 %all_to_all.71.data_ref = f32[8,136,128]{2,1,0:T(8,128)S(1)} all-to-all(f32[8,136,128]{2,1,0:T(8,128)S(1)} %sum_copies.3), channel_id=1, replica_groups=mesh['y'=8,'z'=12,'narrow'=8] {'narrow'}, dimensions={0} | all-to-all | bytes 1114112 | tf_op jit(solution)/shard_map/all_to_all | solution.py:184
  177.8 7.5 %backward.3 = (f32[8,200,128]{2,1,0:T(8,128)S(1)}, f32[16,64,128]{2,1,0:T(8,128)S(1)}) custom-call(s32[128]{0:T(128)S(1)} %copy-done.4, s32[128]{0:T(128)S(1)} %compare_select_fusion.1.dst_ref, f32[8,136,128]{2,1,0:T(8,128)S(1)} %all_to_all.71.data_ref, f32[16,1,128]{2,1,0:T(1,128)S(1)} %bitcast.16, bf16[128,128,128]{2,1,0:T(8,128)(2,1)S(1)} %copy-done.3), custom_call_target="tpu_custom_call" | custom-call | tf_op jit(solution)/shard_map/backward/pallas_call | solution.py:139
  185.3 25.9 %all_to_all.72.got_ref = f32[8,200,128]{2,1,0:T(8,128)S(1)} all-to-all(f32[8,200,128]{2,1,0:T(8,128)S(1)} %get-tuple-element.14), channel_id=1, replica_groups=mesh['y'=8,'z'=12,'narrow'=8] {'y'}, dimensions={0} | all-to-all | bytes 1638400 | tf_op jit(solution)/shard_map/all_to_all | solution.py:184
  211.2 13.1 %all_to_all.73.got_ref = f32[12,24,128]{2,1,0:T(8,128)S(1)} all-to-all(f32[12,24,128]{2,1,0:T(8,128)S(1)} %sum_split.3), channel_id=1, replica_groups=mesh['y'=8,'z'=12,'narrow'=8] {'z'}, dimensions={0} | all-to-all | bytes 294912 | tf_op jit(solution)/shard_map/all_to_all | solution.py:184
  224.3 13.3 %all_to_all.74.got_ref = f32[12,16,128]{2,1,0:T(8,128)S(1)} all-to-all(f32[12,16,128]{2,1,0:T(8,128)S(1)} %get-tuple-element.15), channel_id=1, replica_groups=mesh['y'=8,'z'=12,'narrow'=8] {'z'}, dimensions={0} | all-to-all | bytes 196608 | tf_op jit(solution)/shard_map/all_to_all | solution.py:184
  237.6 0.1 copies.3
  237.7 21.2 %all_to_all.75.data_ref = f32[8,200,128]{2,1,0:T(8,128)S(1)} all-to-all(f32[8,200,128]{2,1,0:T(8,128)S(1)} %copies.3), channel_id=1, replica_groups=mesh['y'=8,'z'=12,'narrow'=8] {'y'}, dimensions={0} | all-to-all | bytes 1638400 | tf_op jit(solution)/shard_map/all_to_all | solution.py:184
  258.9 6.2 %finish_items.1 = (f32[24,64,128]{2,1,0:T(8,128)S(1)}, f32[8,32,128]{2,1,0:T(8,128)}, f32[64,64]{1,0:T(8,128)S(1)}) custom-call(f32[8,200,128]{2,1,0:T(8,128)S(1)} %all_to_all.75.data_ref, f32[24,1,128]{2,1,0:T(1,128)S(1)} %bitcast.14), custom_call_target="tpu_custom_call" | custom-call | tf_op jit(solution)/shard_map/finish_items/pallas_call | solution.py:166
  265.1 9.2 %all-to-all-start.12 = ((f32[8,32,128]{2,1,0:T(8,128)}), f32[8,32,128]{2,1,0:T(8,128)S(1)}, u32[]{:S(2)}, u32[]{:S(2)}) async-start(f32[8,32,128]{2,1,0:T(8,128)} %get-tuple-element.19), calls=%async_computation.12 | async-start | bytes 262144 | tf_op jit(solution)/shard_map/all_to_all | solution.py:184
  274.3 1.3 finish_users.1
  275.7 4.0 %all-to-all-done.12.grams_ref = f32[8,32,128]{2,1,0:T(8,128)S(1)} async-done(((f32[8,32,128]{2,1,0:T(8,128)}), f32[8,32,128]{2,1,0:T(8,128)S(1)}, u32[]{:S(2)}, u32[]{:S(2)}) %all-to-all-start.12) | async-done | bytes 131104 | tf_op jit(solution)/shard_map/all_to_all | solution.py:184
  279.6 3.5 %finish_vectors.1 = f32[64,3072]{1,0:T(8,128)} custom-call(f32[24,64,128]{2,1,0:T(8,128)S(1)} %get-tuple-element.18.raw_ref, f32[8,32,128]{2,1,0:T(8,128)S(1)} %all-to-all-done.12.grams_ref), custom_call_target="tpu_custom_call" | custom-call | tf_op jit(solution)/shard_map/finish_vectors/pallas_call | solution.py:166
  (7 shorter events, 0.2 us)
Async XLA Ops:
  0.6 1.4 copy-start
  2.8 2.2 copy-start.1
  5.0 0.7 copy-start.5
  5.7 32.0 %copy-start.6 = (s32[128]{0:T(128)S(1)}, s32[128]{0:T(128)}, u32[]{:S(2)}) copy-start(s32[128]{0:T(128)} %src_ref.6) | copy-start | bytes 1540
  5.7 32.1 %copy-start.7 = (s32[2048]{0:T(1024)S(1)}, s32[2048]{0:T(1024)}, u32[]{:S(2)}) copy-start(s32[2048]{0:T(1024)} %param.11) | copy-start | bytes 24580
  5.7 41.5 %copy-start.4 = (s32[128]{0:T(128)S(1)}, s32[128]{0:T(128)}, u32[]{:S(2)}) copy-start(s32[128]{0:T(128)} %src_ref.7) | copy-start | bytes 1540
  33.3 13.9 %all-to-all-start.1 = ((f32[8,128,128]{2,1,0:T(8,128)}), f32[8,128,128]{2,1,0:T(8,128)S(1)}, u32[]{:S(2)}, u32[]{:S(2)}) async-start(f32[8,128,128]{2,1,0:T(8,128)} %sum_copies.2), calls=%async_computation.1 | async-start | bytes 1048576 | tf_op jit(solution)/shard_map/all_to_all | solution.py:184
  47.2 2.2 copy-start.2
  53.5 82.7 %copy-start.3 = (bf16[128,128,128]{2,1,0:T(8,128)(2,1)S(1)}, bf16[128,128,128]{2,1,0:T(8,128)(2,1)}, u32[]{:S(2)}) copy-start(bf16[128,128,128]{2,1,0:T(8,128)(2,1)} %tiles_ref.7) | copy-start | bytes 12582916
  265.1 14.5 %all-to-all-start.12 = ((f32[8,32,128]{2,1,0:T(8,128)}), f32[8,32,128]{2,1,0:T(8,128)S(1)}, u32[]{:S(2)}, u32[]{:S(2)}) async-start(f32[8,32,128]{2,1,0:T(8,128)} %get-tuple-element.19), calls=%async_computation.12 | async-start | bytes 262144 | tf_op jit(solution)/shard_map/all_to_all | solution.py:184

commit v3 on v2

v3 whole, which is shorter than its diff:
```python
import math

import jax
import jax.numpy as jnp
from jax import lax
from jax.experimental import pallas as pl
from jax.experimental.pallas import tpu as pltpu
from jax.sharding import Mesh, PartitionSpec as P

ITERS = 2
GROUP = 16
Y_CHIPS = 8
Z_PAIR = 2
SUB = 8
WIDTH = 4
FULL = lax.Precision.HIGHEST
VMEM = pl.BlockSpec(memory_space=pltpu.VMEM)


def dot(a, b, last=False):
    dims = (((1,), (1,)), ((), ())) if last else (((1,), (0,)), ((), ()))
    return lax.dot_general(a, b, dims, precision=FULL, preferred_element_type=jnp.float32)


def inverse_factor(panels):
    vectors = len(panels) * SUB
    lane = lax.broadcasted_iota(jnp.int32, (SUB, 2 * vectors), 1)
    sub = lax.broadcasted_iota(jnp.int32, (SUB, 2 * vectors), 0)
    rows = []
    for p, panel in enumerate(panels):
        unit = jnp.where(lane == vectors + p * SUB + sub, 1.0, 0.0)
        rows.append(jnp.where(lane < vectors, panel, unit))

    def spread(panel, p):
        return [jnp.broadcast_to(panel[:, p * SUB + q : p * SUB + q + 1], panel.shape) for q in range(SUB)]

    def row(value, q):
        return jnp.broadcast_to(value[q : q + 1, :], value.shape)

    for p in range(len(panels)):
        cols = spread(rows[p], p)
        pivots, heads, inverses = [], [], []
        scale = jnp.ones_like(rows[p])
        for q in range(SUB):
            head = row(rows[p], q)
            tops = [None if t < q else row(cols[t], q) for t in range(SUB)]
            inverse = 1.0 / tops[q]
            pivots.append(head)
            heads.append(tops)
            inverses.append(inverse)
            scale = jnp.where(sub == q, tops[q], scale)
            factor = jnp.where(sub > q, cols[q] * inverse, 0.0)
            rows[p] = rows[p] - factor * head
            for t in range(q + 1, SUB):
                cols[t] = cols[t] - factor * tops[t]
        for r in range(p + 1, len(panels)):
            cols = spread(rows[r], p)
            for q in range(SUB):
                factor = cols[q] * inverses[q]
                rows[r] = rows[r] - factor * pivots[q]
                for t in range(q + 1, SUB):
                    cols[t] = cols[t] - factor * heads[q][t]
        rows[p] = rows[p] * lax.rsqrt(scale)
    return jnp.concatenate(rows, axis=0)[:, vectors:]


def padded(gram):
    return jnp.concatenate([gram, jnp.zeros_like(gram)], axis=1)


def read_block(ref, block, vectors, per_chunk):
    part = math.gcd(vectors, per_chunk)
    pieces = []
    for row in range(block * vectors, (block + 1) * vectors, part):
        at = row % per_chunk
        pieces.append(ref[row // per_chunk, at : at + part, :])
    return pieces[0] if len(pieces) == 1 else jnp.concatenate(pieces, axis=0)


def write_block(ref, block, value, per_chunk):
    vectors = value.shape[0]
    part = math.gcd(vectors, per_chunk)
    for begin in range(0, vectors, part):
        row = block * vectors + begin
        at = row % per_chunk
        ref[row // per_chunk, at : at + part, :] = value[begin : begin + part]


def gram_panels(ref, per_chunk, vectors, count):
    return [ref[c, per_chunk : per_chunk + SUB, :] * (1.0 / count) for c in range(vectors // SUB)]


def scale_of(degree):
    return lax.rsqrt(degree.astype(jnp.float32))


def phase(data, degree, tiles, src, dst, used, blocks_out, out_chunks, forward, gram_count, send_gram, keep_raw):
    slots, tile, _ = tiles.shape
    blocks = degree.shape[0]
    begins = data.ndim == 2
    vectors = data.shape[0] if begins else tile // 2
    per_chunk = None if begins else blocks * vectors // data.shape[0]
    have_gram = gram_count is not None
    terms = 1 if begins else 2
    out_per = blocks_out * vectors // out_chunks
    out_rows = out_per + (SUB if send_gram else 0)
    steps = slots // GROUP
    dims = (((1,), (1,)), ((), ())) if forward else (((1,), (0,)), ((), ()))

    def body(src_ref, dst_ref, used_ref, data_ref, degree_ref, tiles_ref, out_ref, *rest):
        if keep_raw:
            raw_ref, x_ref, sums_ref, gram_ref = rest
        else:
            x_ref, sums_ref, gram_ref = rest
        step = pl.program_id(0)

        @pl.when(step == 0)
        def _():
            sums_ref[...] = jnp.zeros_like(sums_ref)
            if have_gram:
                inverse = inverse_factor(gram_panels(data_ref, per_chunk, vectors, gram_count))
            gram = jnp.zeros((vectors, vectors), jnp.float32)
            for first in range(0, blocks, WIDTH):
                group = range(first, first + WIDTH)
                weight = jnp.concatenate([scale_of(degree_ref[block]) for block in group], axis=1)
                if begins:
                    raw = data_ref[:, first * tile : (first + WIDTH) * tile]
                else:
                    raw = jnp.concatenate([read_block(data_ref, block, vectors, per_chunk) for block in group], axis=1)
                    if have_gram:
                        raw = dot(inverse, raw)
                    raw = raw * weight
                if send_gram:
                    gram = gram + dot(raw, raw, last=True)
                source = raw * weight
                high = source.astype(jnp.bfloat16)
                if terms == 2:
                    low = (source - high.astype(jnp.float32)).astype(jnp.bfloat16)
                for at, block in enumerate(group):
                    lanes = slice(at * tile, (at + 1) * tile)
                    x_ref[block, :vectors, :] = high[:, lanes]
                    if terms == 2:
                        x_ref[block, vectors:, :] = low[:, lanes]
                    if keep_raw:
                        raw_ref[block] = raw[:, lanes]
            if send_gram:
                gram_ref[...] = padded(gram)

        for slot in range(GROUP):
            at = step * GROUP + slot
            product = lax.dot_general(
                x_ref[src_ref[at]], tiles_ref[slot], dims, preferred_element_type=jnp.float32
            )
            if terms == 2:
                product = product[:vectors] + product[vectors:]
            sums_ref[jnp.where(at < used_ref[0], dst_ref[at], blocks_out)] += product

        @pl.when(step == steps - 1)
        def _():
            for block in range(blocks_out):
                write_block(out_ref, block, sums_ref[block], out_per)
            if send_gram:
                for c in range(out_chunks):
                    rows = gram_ref[c * SUB : (c + 1) * SUB, :] if c * SUB < vectors else jnp.zeros((SUB, tile), jnp.float32)
                    out_ref[c, out_per:, :] = rows

    out_shape = [jax.ShapeDtypeStruct((out_chunks, out_rows, tile), jnp.float32)]
    out_specs = [pl.BlockSpec((out_chunks, out_rows, tile), lambda i, *_: (0, 0, 0))]
    if keep_raw:
        out_shape.append(jax.ShapeDtypeStruct((blocks, vectors, tile), jnp.float32))
        out_specs.append(pl.BlockSpec((blocks, vectors, tile), lambda i, *_: (0, 0, 0)))
    return pl.pallas_call(
        body,
        grid_spec=pltpu.PrefetchScalarGridSpec(
            num_scalar_prefetch=3,
            grid=(steps,),
            in_specs=[
                pl.BlockSpec(data.shape, lambda i, *_: (0,) * data.ndim),
                pl.BlockSpec(degree.shape, lambda i, *_: (0, 0, 0)),
                pl.BlockSpec((GROUP, tile, tile), lambda i, *_: (i, 0, 0)),
            ],
            out_specs=out_specs,
            scratch_shapes=[
                pltpu.VMEM((blocks, terms * vectors, tile), jnp.bfloat16),
                pltpu.VMEM((blocks_out + 1, vectors, tile), jnp.float32),
                pltpu.VMEM((vectors, tile), jnp.float32),
            ],
        ),
        out_shape=out_shape,
        compiler_params=pltpu.CompilerParams(vmem_limit_bytes=PHASE_LIMIT),
        name="forward" if forward else "backward",
    )(src, dst, used, data, degree, tiles)


PHASE_LIMIT = 60 * 1024 * 1024
VMEM_LIMIT = 32 * 1024 * 1024


def call(body, inputs, shapes, name):
    return pl.pallas_call(
        body,
        in_specs=[VMEM] * len(inputs),
        out_specs=[VMEM] * len(shapes),
        out_shape=[jax.ShapeDtypeStruct(s, jnp.float32) for s in shapes],
        compiler_params=pltpu.CompilerParams(vmem_limit_bytes=VMEM_LIMIT),
        name=name,
    )(*inputs)


def total(ref, begin, end):
    value = ref[0, begin:end, :]
    for c in range(1, ref.shape[0]):
        value = value + ref[c, begin:end, :]
    return value


def exchange(data, axis):
    return lax.all_to_all(data, axis, 0, 0)


def sum_copies(got, copies):
    def body(got_ref, out_ref):
        mine = total(got_ref, 0, got_ref.shape[1])
        for c in range(copies):
            out_ref[c] = mine

    return call(body, [got], [(copies,) + got.shape[1:]], "sum_copies")[0]


def narrow_sum(chunks):
    return exchange(sum_copies(exchange(chunks, "narrow"), chunks.shape[0]), "narrow")


def wide_sum(chunks):
    near = ("y", "z_low")
    part = sum_copies(exchange(chunks, near), lax.axis_size("z_high"))
    return exchange(sum_copies(exchange(part, "z_high"), chunks.shape[0]), near)


def finish_items(data, degree, user_count, copies):
    chunks, _, tile = data.shape
    blocks = degree.shape[0]
    vectors = tile // 2
    per_chunk = blocks * vectors // chunks

    def body(data_ref, degree_ref, raw_ref, gram_ref, inverse_ref):
        inverse = inverse_factor(gram_panels(data_ref, per_chunk, vectors, user_count))
        inverse_ref[...] = inverse
        gram = jnp.zeros((vectors, vectors), jnp.float32)
        for first in range(0, blocks, WIDTH):
            group = range(first, first + WIDTH)
            weight = jnp.concatenate([scale_of(degree_ref[block]) for block in group], axis=1)
            raw = jnp.concatenate([read_block(data_ref, block, vectors, per_chunk) for block in group], axis=1)
            raw = dot(inverse, raw) * weight
            gram = gram + dot(raw, raw, last=True)
            raw_ref[:, first * tile : (first + WIDTH) * tile] = raw
        packed = jnp.concatenate([gram[: vectors // 2], gram[vectors // 2 :]], axis=1)
        for c in range(copies):
            gram_ref[c] = packed

    shapes = [(vectors, blocks * tile), (copies, vectors // 2, tile), (vectors, vectors)]
    return call(body, [data, degree], shapes, "finish_items")


def finish_users(raw, inverse):
    blocks, vectors, tile = raw.shape

    def body(raw_ref, inverse_ref, out_ref):
        for block in range(blocks):
            out_ref[:, block * tile : (block + 1) * tile] = dot(inverse_ref[...], raw_ref[block])

    return call(body, [raw, inverse], [(vectors, blocks * tile)], "finish_users")[0]


def finish_vectors(raw, grams, item_count):
    vectors, rows = raw.shape
    width = WIDTH * grams.shape[2]

    def body(raw_ref, grams_ref, out_ref):
        gram = total(grams_ref, 0, vectors // 2) * (1.0 / item_count)
        gram = jnp.concatenate([gram[:, :vectors], gram[:, vectors:]], axis=0)
        gram = padded(gram)
        inverse = inverse_factor([gram[at : at + SUB] for at in range(0, vectors, SUB)])
        for begin in range(0, rows, width):
            out_ref[:, begin : begin + width] = dot(inverse, raw_ref[:, begin : begin + width])

    return call(body, [raw, grams], [raw.shape], "finish_vectors")[0]


def local(tile_values, tile_row, tile_col, tile_count, user_degree, item_degree, start_vectors):
    vectors, item_rows = start_vectors.shape
    slot_count, tile, _ = tile_values.shape
    user_rows = user_degree.shape[0]
    user_blocks = user_rows // tile
    item_blocks = item_rows // tile
    narrow_count = lax.axis_size("narrow")
    near_count = lax.axis_size("y") * lax.axis_size("z_low")
    all_users = user_rows * near_count * lax.axis_size("z_high")
    all_items = item_rows * narrow_count
    users = user_degree.reshape(user_blocks, 1, tile)
    items = item_degree.reshape(item_blocks, 1, tile)

    item_data = start_vectors
    for step in range(ITERS):
        first, last = step == 0, step == ITERS - 1
        (terms,) = phase(
            item_data, items, tile_values, tile_col, tile_row, tile_count, user_blocks, narrow_count, True,
            None if first else all_users, not first, False,
        )
        user_data = narrow_sum(terms)
        out = phase(
            user_data, users, tile_values, tile_row, tile_col, tile_count, item_blocks, near_count, False,
            None if first else all_items, True, last,
        )
        item_data = wide_sum(out[0])
    user_raw = out[1]
    item_raw, grams, user_inverse = finish_items(item_data, items, all_users, narrow_count)
    grams = exchange(grams, "narrow")
    user_vectors = finish_users(user_raw, user_inverse)
    item_vectors = finish_vectors(item_raw, grams, all_items)
    return (user_vectors, item_vectors)


def solution(mesh):
    wide_count, narrow_count = mesh.devices.shape
    grid = mesh.devices.reshape(Y_CHIPS, wide_count // (Y_CHIPS * Z_PAIR), Z_PAIR, narrow_count)
    wide = ("y", "z_high", "z_low")
    owner = wide + ("narrow",)
    return jax.shard_map(
        local,
        mesh=Mesh(grid, owner),
        in_specs=(
            P(owner, None, None),
            P(owner),
            P(owner),
            P(owner),
            P(wide),
            P("narrow"),
            P(None, "narrow"),
        ),
        out_specs=(P(None, wide), P(None, "narrow")),
        check_vma=False,
    )
```

time: 284 us -> 281 us (0.989)
  Pallas kernels: 38.2 us -> 49.4 us
  blocking collectives: 210 us -> 220 us
  waiting for transfers between devices: 13.4 us -> 3.95 us
  starting transfers between devices: 13.6 us -> 4.73 us
  local copies, waits for them, and re-layouts: 5.14 us -> 0.01 us
    pallas_call x4, Pallas kernels: 26 us -> 40 us  [phase(): pl.pallas_call(body, grid_spec=pltpu.PrefetchScalarGridSpec(num_scalar_pr...]
    all_to_all x11 -> x10, blocking collectives: 210 us -> 220 us  [exchange(): return lax.all_to_all(data, axis, 0, 0)]
    all_to_all x2 -> x1, waiting for transfers between devices: 13.4 us -> 3.95 us  [exchange(): return lax.all_to_all(data, axis, 0, 0)]
    all_to_all x2 -> x1, starting transfers between devices: 13.6 us -> 4.73 us  [exchange(): return lax.all_to_all(data, axis, 0, 0)]
    unnamed x16 -> x4, local copies, waits for them, and re-layouts: 5.06 us -> 0.01 us
    pallas_call x11 -> x9, Pallas kernels: 12.2 us -> 9.42 us  [call(): pl.pallas_call(body, in_specs=[VMEM] * len(inputs), out_specs=[VMEM] * le...]
  transfers between devices with their start and end apart: 2 -> 1, of which waited for: 2 -> 1; matrix products, arithmetic and copies ran while one was open for 0% -> 0% of each run, Pallas kernels for 0% -> 0%
where the time goes in v3:
time: 281 us; the launch traced here: 279 us
  blocking collectives  220 us (78%)
  Pallas kernels  49.4 us (18%)
  starting transfers between devices  4.73 us (2%)
  waiting for transfers between devices  3.95 us (1%)
    all_to_all x10, blocking collectives, exchange(): return lax.all_to_all(data, axis, 0, 0)  220 us
    pallas_call x4, Pallas kernels, phase(): pl.pallas_call(body, grid_spec=pltpu.PrefetchScalarGridSpec(num_scalar_pr...  40 us
    pallas_call x9, Pallas kernels, call(): pl.pallas_call(body, in_specs=[VMEM] * len(inputs), out_specs=[VMEM] * le...  9.42 us
  transfers between devices with their start and end apart: 1, of which 1 were waited for; matrix products, arithmetic and copies ran while one was open for 0% of the time, Pallas kernels for 0%

profile of v3, /device:TPU:1, one launch (start us, length us, event | category | flops | bytes accessed | tf_op | source)
XLA Modules:
  0.0 279.5 jit_solution(16992099451316373384)
XLA Ops:
  1.3 8.5 %forward.2 = f32[8,128,128]{2,1,0:T(8,128)} custom-call(s32[128]{0:T(128)} %dst_ref.7, s32[128]{0:T(128)} %src_ref.7, s32[1]{0:T(128)S(6)} %copy.9.used_ref, f32[64,3072]{1,0:T(8,128)} %data_ref.1, s32[24,1,128]{2,1,0:T(1,128)} %bitcast.2, bf16[128,128,128]{2,1,0:T(8,128)(2,1)} %tiles_ref.7), custom_call_target="tpu_custom_call" | custom-call | tf_op jit(solution)/shard_map/forward/pallas_call | solution.py:172
  9.8 23.3 %all_to_all.55.got_ref = f32[8,128,128]{2,1,0:T(8,128)S(1)} all-to-all(f32[8,128,128]{2,1,0:T(8,128)} %forward.2), channel_id=1, replica_groups=mesh['y'=8,'z_high'=6,'z_low'=2,'narrow'=8] {'narrow'}, dimensions={0} | all-to-all | bytes 1048576 | tf_op jit(solution)/shard_map/all_to_all | solution.py:218
  33.1 13.5 %all_to_all.56.data_ref = f32[8,128,128]{2,1,0:T(8,128)} all-to-all(f32[8,128,128]{2,1,0:T(8,128)S(1)} %sum_copies.6), channel_id=1, replica_groups=mesh['y'=8,'z_high'=6,'z_low'=2,'narrow'=8] {'narrow'}, dimensions={0} | all-to-all | bytes 1048576 | tf_op jit(solution)/shard_map/all_to_all | solution.py:218
  46.6 8.3 %backward.2 = f32[16,104,128]{2,1,0:T(8,128)} custom-call(s32[128]{0:T(128)} %src_ref.7, s32[128]{0:T(128)} %dst_ref.7, s32[1]{0:T(128)S(6)} %copy.9.used_ref, f32[8,128,128]{2,1,0:T(8,128)} %all_to_all.56.data_ref, s32[16,1,128]{2,1,0:T(1,128)} %bitcast.5, bf16[128,128,128]{2,1,0:T(8,128)(2,1)} %tiles_ref.7), custom_call_target="tpu_custom_call" | custom-call | tf_op jit(solution)/shard_map/backward/pallas_call | solution.py:172
  54.9 26.0 %all_to_all.57.got_ref = f32[16,104,128]{2,1,0:T(8,128)S(1)} all-to-all(f32[16,104,128]{2,1,0:T(8,128)} %backward.2), channel_id=1, replica_groups=mesh['y'=8,'z_high'=6,'z_low'=2,'narrow'=8] {'y','z_low'}, dimensions={0} | all-to-all | bytes 1703936 | tf_op jit(solution)/shard_map/all_to_all | solution.py:218
  80.9 0.1 sum_copies.7
  81.0 23.2 %all_to_all.58.got_ref = f32[6,104,128]{2,1,0:T(8,128)S(1)} all-to-all(f32[6,104,128]{2,1,0:T(8,128)S(1)} %sum_copies.7), channel_id=1, replica_groups=mesh['y'=8,'z_high'=6,'z_low'=2,'narrow'=8] {'z_high'}, dimensions={0} | all-to-all | bytes 638976 | tf_op jit(solution)/shard_map/all_to_all | solution.py:218
  104.1 0.1 sum_copies.8
  104.2 30.7 %all_to_all.59.data_ref = f32[16,104,128]{2,1,0:T(8,128)} all-to-all(f32[16,104,128]{2,1,0:T(8,128)S(1)} %sum_copies.8), channel_id=1, replica_groups=mesh['y'=8,'z_high'=6,'z_low'=2,'narrow'=8] {'y','z_low'}, dimensions={0} | all-to-all | bytes 1703936 | tf_op jit(solution)/shard_map/all_to_all | solution.py:218
  134.9 12.1 %forward.3 = f32[8,136,128]{2,1,0:T(8,128)} custom-call(s32[128]{0:T(128)} %dst_ref.7, s32[128]{0:T(128)} %src_ref.7, s32[1]{0:T(128)S(6)} %copy.9.used_ref, f32[16,104,128]{2,1,0:T(8,128)} %all_to_all.59.data_ref, s32[24,1,128]{2,1,0:T(1,128)} %bitcast.3, bf16[128,128,128]{2,1,0:T(8,128)(2,1)} %tiles_ref.7), custom_call_target="tpu_custom_call" | custom-call | tf_op jit(solution)/shard_map/forward/pallas_call | solution.py:172
  147.1 15.1 %all_to_all.60.got_ref = f32[8,136,128]{2,1,0:T(8,128)S(1)} all-to-all(f32[8,136,128]{2,1,0:T(8,128)} %forward.3), channel_id=1, replica_groups=mesh['y'=8,'z_high'=6,'z_low'=2,'narrow'=8] {'narrow'}, dimensions={0} | all-to-all | bytes 1114112 | tf_op jit(solution)/shard_map/all_to_all | solution.py:218
  162.2 13.8 %all_to_all.61.data_ref = f32[8,136,128]{2,1,0:T(8,128)} all-to-all(f32[8,136,128]{2,1,0:T(8,128)S(1)} %sum_copies.9), channel_id=1, replica_groups=mesh['y'=8,'z_high'=6,'z_low'=2,'narrow'=8] {'narrow'}, dimensions={0} | all-to-all | bytes 1114112 | tf_op jit(solution)/shard_map/all_to_all | solution.py:218
  176.1 11.0 %backward.3 = (f32[16,104,128]{2,1,0:T(8,128)}, f32[16,64,128]{2,1,0:T(8,128)}) custom-call(s32[128]{0:T(128)} %src_ref.7, s32[128]{0:T(128)} %dst_ref.7, s32[1]{0:T(128)S(6)} %copy.9.used_ref, f32[8,136,128]{2,1,0:T(8,128)} %all_to_all.61.data_ref, s32[16,1,128]{2,1,0:T(1,128)} %bitcast.6, bf16[128,128,128]{2,1,0:T(8,128)(2,1)} %tiles_ref.7), custom_call_target="tpu_custom_call" | custom-call | tf_op jit(solution)/shard_map/backward/pallas_call | solution.py:172
  187.1 0.0 copy-start.1
  187.1 0.0 copy-start
  187.1 26.4 %all_to_all.62.got_ref = f32[16,104,128]{2,1,0:T(8,128)S(1)} all-to-all(f32[16,104,128]{2,1,0:T(8,128)} %get-tuple-element.8), channel_id=1, replica_groups=mesh['y'=8,'z_high'=6,'z_low'=2,'narrow'=8] {'y','z_low'}, dimensions={0} | all-to-all | bytes 1703936 | tf_op jit(solution)/shard_map/all_to_all | solution.py:218
  213.5 0.1 sum_copies.10
  213.6 17.0 %all_to_all.63.got_ref = f32[6,104,128]{2,1,0:T(8,128)S(1)} all-to-all(f32[6,104,128]{2,1,0:T(8,128)S(1)} %sum_copies.10), channel_id=1, replica_groups=mesh['y'=8,'z_high'=6,'z_low'=2,'narrow'=8] {'z_high'}, dimensions={0} | all-to-all | bytes 638976 | tf_op jit(solution)/shard_map/all_to_all | solution.py:218
  230.5 0.1 sum_copies.11
  230.6 31.0 %all_to_all.64.data_ref = f32[16,104,128]{2,1,0:T(8,128)S(1)} all-to-all(f32[16,104,128]{2,1,0:T(8,128)S(1)} %sum_copies.11), channel_id=1, replica_groups=mesh['y'=8,'z_high'=6,'z_low'=2,'narrow'=8] {'y','z_low'}, dimensions={0} | all-to-all | bytes 1703936 | tf_op jit(solution)/shard_map/all_to_all | solution.py:218
  261.7 0.0 copy-done.1
  261.7 4.3 %finish_items.1 = (f32[64,3072]{1,0:T(8,128)S(1)}, f32[8,32,128]{2,1,0:T(8,128)}, f32[64,64]{1,0:T(8,128)S(1)}) custom-call(f32[16,104,128]{2,1,0:T(8,128)S(1)} %all_to_all.64.data_ref, s32[24,1,128]{2,1,0:T(1,128)S(1)} %bitcast.4), custom_call_target="tpu_custom_call" | custom-call | tf_op jit(solution)/shard_map/finish_items/pallas_call | solution.py:200
  266.0 4.7 %all-to-all-start.10 = ((f32[8,32,128]{2,1,0:T(8,128)}), f32[8,32,128]{2,1,0:T(8,128)S(1)}, u32[]{:S(2)}, u32[]{:S(2)}) async-start(f32[8,32,128]{2,1,0:T(8,128)} %get-tuple-element.11), calls=%async_computation.10 | async-start | bytes 262144 | tf_op jit(solution)/shard_map/all_to_all | solution.py:218
  270.7 0.0 copy-done
  270.7 1.3 finish_users.1
  272.0 4.0 %all-to-all-done.10.grams_ref = f32[8,32,128]{2,1,0:T(8,128)S(1)} async-done(((f32[8,32,128]{2,1,0:T(8,128)}), f32[8,32,128]{2,1,0:T(8,128)S(1)}, u32[]{:S(2)}, u32[]{:S(2)}) %all-to-all-start.10) | async-done | bytes 131104 | tf_op jit(solution)/shard_map/all_to_all | solution.py:218
  276.0 3.5 %finish_vectors.1 = f32[64,3072]{1,0:T(8,128)} custom-call(f32[64,3072]{1,0:T(8,128)S(1)} %get-tuple-element.10.raw_ref, f32[8,32,128]{2,1,0:T(8,128)S(1)} %all-to-all-done.10.grams_ref), custom_call_target="tpu_custom_call" | custom-call | tf_op jit(solution)/shard_map/finish_vectors/pallas_call | solution.py:200
  (2 shorter events, 0.1 us)
Async XLA Ops:
  187.1 74.6 %copy-start.1 = (s32[3072]{0:T(1024)S(1)}, s32[3072]{0:T(1024)}, u32[]{:S(2)}) copy-start(s32[3072]{0:T(1024)} %param.12) | copy-start | bytes 36868
  187.1 83.6 %copy-start = (f32[16,64,128]{2,1,0:T(8,128)S(1)}, f32[16,64,128]{2,1,0:T(8,128)}, u32[]{:S(2)}) copy-start(f32[16,64,128]{2,1,0:T(8,128)} %get-tuple-element.7.raw_ref) | copy-start | bytes 1572868
  266.0 10.0 %all-to-all-start.10 = ((f32[8,32,128]{2,1,0:T(8,128)}), f32[8,32,128]{2,1,0:T(8,128)S(1)}, u32[]{:S(2)}, u32[]{:S(2)}) async-start(f32[8,32,128]{2,1,0:T(8,128)} %get-tuple-element.11), calls=%async_computation.10 | async-start | bytes 262144 | tf_op jit(solution)/shard_map/all_to_all | solution.py:218

commit v4 on v3

--- a/solution.py
+++ b/solution.py
@@ -13,8 +13,10 @@
 Z_PAIR = 2
 SUB = 8
 WIDTH = 4
+VMEM_LIMIT = 16 * 1024 * 1024
 FULL = lax.Precision.HIGHEST
 VMEM = pl.BlockSpec(memory_space=pltpu.VMEM)
+SMEM = pl.BlockSpec(memory_space=pltpu.SMEM)
 
 
 def dot(a, b, last=False):
@@ -104,96 +106,75 @@
     terms = 1 if begins else 2
     out_per = blocks_out * vectors // out_chunks
     out_rows = out_per + (SUB if send_gram else 0)
-    steps = slots // GROUP
     dims = (((1,), (1,)), ((), ())) if forward else (((1,), (0,)), ((), ()))
 
     def body(src_ref, dst_ref, used_ref, data_ref, degree_ref, tiles_ref, out_ref, *rest):
         if keep_raw:
-            raw_ref, x_ref, sums_ref, gram_ref = rest
+            raw_ref, x_ref, sums_ref = rest
         else:
-            x_ref, sums_ref, gram_ref = rest
-        step = pl.program_id(0)
-
-        @pl.when(step == 0)
-        def _():
-            sums_ref[...] = jnp.zeros_like(sums_ref)
-            if have_gram:
-                inverse = inverse_factor(gram_panels(data_ref, per_chunk, vectors, gram_count))
-            gram = jnp.zeros((vectors, vectors), jnp.float32)
-            for first in range(0, blocks, WIDTH):
-                group = range(first, first + WIDTH)
-                weight = jnp.concatenate([scale_of(degree_ref[block]) for block in group], axis=1)
-                if begins:
-                    raw = data_ref[:, first * tile : (first + WIDTH) * tile]
-                else:
-                    raw = jnp.concatenate([read_block(data_ref, block, vectors, per_chunk) for block in group], axis=1)
-                    if have_gram:
-                        raw = dot(inverse, raw)
-                    raw = raw * weight
-                if send_gram:
-                    gram = gram + dot(raw, raw, last=True)
-                source = raw * weight
-                high = source.astype(jnp.bfloat16)
+            x_ref, sums_ref = rest
+        sums_ref[...] = jnp.zeros_like(sums_ref)
+        if have_gram:
+            inverse = inverse_factor(gram_panels(data_ref, per_chunk, vectors, gram_count))
+        gram = jnp.zeros((vectors, vectors), jnp.float32)
+        for first in range(0, blocks, WIDTH):
+            group = range(first, first + WIDTH)
+            weight = jnp.concatenate([scale_of(degree_ref[block]) for block in group], axis=1)
+            if begins:
+                raw = data_ref[:, first * tile : (first + WIDTH) * tile]
+            else:
+                raw = jnp.concatenate([read_block(data_ref, block, vectors, per_chunk) for block in group], axis=1)
+                if have_gram:
+                    raw = dot(inverse, raw)
+                raw = raw * weight
+            if send_gram:
+                gram = gram + dot(raw, raw, last=True)
+            source = raw * weight
+            high = source.astype(jnp.bfloat16)
+            if terms == 2:
+                low = (source - high.astype(jnp.float32)).astype(jnp.bfloat16)
+            for at, block in enumerate(group):
+                lanes = slice(at * tile, (at + 1) * tile)
+                x_ref[block, :vectors, :] = high[:, lanes]
                 if terms == 2:
-                    low = (source - high.astype(jnp.float32)).astype(jnp.bfloat16)
-                for at, block in enumerate(group):
-                    lanes = slice(at * tile, (at + 1) * tile)
-                    x_ref[block, :vectors, :] = high[:, lanes]
-                    if terms == 2:
-                        x_ref[block, vectors:, :] = low[:, lanes]
-                    if keep_raw:
-                        raw_ref[block] = raw[:, lanes]
-            if send_gram:
-                gram_ref[...] = padded(gram)
-
-        for slot in range(GROUP):
-            at = step * GROUP + slot
-            product = lax.dot_general(
-                x_ref[src_ref[at]], tiles_ref[slot], dims, preferred_element_type=jnp.float32
-            )
-            if terms == 2:
-                product = product[:vectors] + product[vectors:]
-            sums_ref[jnp.where(at < used_ref[0], dst_ref[at], blocks_out)] += product
-
-        @pl.when(step == steps - 1)
-        def _():
-            for block in range(blocks_out):
-                write_block(out_ref, block, sums_ref[block], out_per)
-            if send_gram:
-                for c in range(out_chunks):
-                    rows = gram_ref[c * SUB : (c + 1) * SUB, :] if c * SUB < vectors else jnp.zeros((SUB, tile), jnp.float32)
-                    out_ref[c, out_per:, :] = rows
+                    x_ref[block, vectors:, :] = low[:, lanes]
+                if keep_raw:
+                    raw_ref[block] = raw[:, lanes]
+        if send_gram:
+            both = padded(gram)
+            for c in range(out_chunks):
+                inside = c * SUB < vectors
+                out_ref[c, out_per:, :] = both[c * SUB : (c + 1) * SUB] if inside else jnp.zeros((SUB, tile), jnp.float32)
+
+        @pl.loop(0, slots // GROUP)
+        def _(step):
+            for slot in range(GROUP):
+                at = step * GROUP + slot
+                product = lax.dot_general(
+                    x_ref[src_ref[at]], tiles_ref[at], dims, preferred_element_type=jnp.float32
+                )
+                if terms == 2:
+                    product = product[:vectors] + product[vectors:]
+                sums_ref[jnp.where(at < used_ref[0], dst_ref[at], blocks_out)] += product
+
+        for block in range(blocks_out):
+            write_block(out_ref, block, sums_ref[block], out_per)
 
     out_shape = [jax.ShapeDtypeStruct((out_chunks, out_rows, tile), jnp.float32)]
-    out_specs = [pl.BlockSpec((out_chunks, out_rows, tile), lambda i, *_: (0, 0, 0))]
     if keep_raw:
         out_shape.append(jax.ShapeDtypeStruct((blocks, vectors, tile), jnp.float32))
-        out_specs.append(pl.BlockSpec((blocks, vectors, tile), lambda i, *_: (0, 0, 0)))
     return pl.pallas_call(
         body,
-        grid_spec=pltpu.PrefetchScalarGridSpec(
-            num_scalar_prefetch=3,
-            grid=(steps,),
-            in_specs=[
-                pl.BlockSpec(data.shape, lambda i, *_: (0,) * data.ndim),
-                pl.BlockSpec(degree.shape, lambda i, *_: (0, 0, 0)),
-                pl.BlockSpec((GROUP, tile, tile), lambda i, *_: (i, 0, 0)),
-            ],
-            out_specs=out_specs,
-            scratch_shapes=[
-                pltpu.VMEM((blocks, terms * vectors, tile), jnp.bfloat16),
-                pltpu.VMEM((blocks_out + 1, vectors, tile), jnp.float32),
-                pltpu.VMEM((vectors, tile), jnp.float32),
-            ],
-        ),
+        in_specs=[SMEM] * 3 + [VMEM] * 3,
+        out_specs=[VMEM] * len(out_shape),
+        scratch_shapes=[
+            pltpu.VMEM((blocks, terms * vectors, tile), jnp.bfloat16),
+            pltpu.VMEM((blocks_out + 1, vectors, tile), jnp.float32),
+        ],
         out_shape=out_shape,
-        compiler_params=pltpu.CompilerParams(vmem_limit_bytes=PHASE_LIMIT),
+        compiler_params=pltpu.CompilerParams(vmem_limit_bytes=VMEM_LIMIT),
         name="forward" if forward else "backward",
     )(src, dst, used, data, degree, tiles)
-
-
-PHASE_LIMIT = 60 * 1024 * 1024
-VMEM_LIMIT = 32 * 1024 * 1024
 
 
 def call(body, inputs, shapes, name):

time: 281 us -> 265 us (0.943)
  Pallas kernels: 49.4 us -> 31.7 us
  local copies, waits for them, and re-layouts: 0.01 us -> 5.35 us
  blocking collectives: 220 us -> 217 us
    pallas_call x4, Pallas kernels: 40 us -> 22.3 us  [phase(): pl.pallas_call(body, in_specs=[SMEM] * 3 + [VMEM] * 3, out_specs=[VMEM] *...]
    unnamed x4 -> x20, local copies, waits for them, and re-layouts: 0.01 us -> 5.35 us
    all_to_all x10, blocking collectives: 220 us -> 217 us  [exchange(): return lax.all_to_all(data, axis, 0, 0)]
  transfers between devices with their start and end apart: 1 -> 1, of which waited for: 1 -> 1; matrix products, arithmetic and copies ran while one was open for 0% -> 0% of each run, Pallas kernels for 0% -> 1%
where the time goes in v4:
time: 265 us; the launch traced here: 264 us
  blocking collectives  217 us (82%)
  Pallas kernels  31.7 us (12%)
  local copies, waits for them, and re-layouts  5.35 us (2%)
  starting transfers between devices  4.76 us (2%)
  waiting for transfers between devices  3.95 us (1%)
    all_to_all x10, blocking collectives, exchange(): return lax.all_to_all(data, axis, 0, 0)  217 us
    pallas_call x4, Pallas kernels, phase(): pl.pallas_call(body, in_specs=[SMEM] * 3 + [VMEM] * 3, out_specs=[VMEM] *...  22.3 us
    pallas_call x9, Pallas kernels, call(): pl.pallas_call(body, in_specs=[VMEM] * len(inputs), out_specs=[VMEM] * le...  9.42 us
    unnamed x20, local copies, waits for them, and re-layouts  5.35 us
  transfers between devices with their start and end apart: 1, of which 1 were waited for; matrix products, arithmetic and copies ran while one was open for 0% of the time, Pallas kernels for 1%

profile of v4, /device:TPU:1, one launch (start us, length us, event | category | flops | bytes accessed | tf_op | source)
XLA Modules:
  0.0 263.8 jit_solution(7211747309237800617)
XLA Ops:
  1.3 0.0 copy-start
  1.3 2.2 copy-done
  3.5 0.0 copy-start.2
  3.5 1.1 copy-done.2
  4.6 0.0 copy-start.3
  4.6 0.7 copy-done.3
  5.3 0.0 copy-start.6
  5.3 0.7 copy-done.6
  6.0 0.0 copy-start.8
  6.0 0.7 copy-done.8
  6.6 0.0 copy-start.1
  6.6 0.0 copy-start.5
  6.6 0.0 copy-start.7
  6.6 0.0 copy-start.9
  6.6 4.4 %forward.2 = f32[8,128,128]{2,1,0:T(8,128)S(1)} custom-call(s32[128]{0:T(128)S(1)} %copy-done.8, s32[128]{0:T(128)S(1)} %copy-done.6, s32[1]{0:T(128)S(6)} %copy.9.used_ref, f32[64,3072]{1,0:T(8,128)S(1)} %copy-done.2, s32[24,1,128]{2,1,0:T(1,128)S(1)} %bitcast.2, bf16[128,128,128]{2,1,0:T(8,128)(2,1)S(1)} %copy-done), custom_call_target="tpu_custom_call" | custom-call | tf_op jit(solution)/shard_map/forward/pallas_call | solution.py:166
  11.0 22.2 %all_to_all.55.got_ref = f32[8,128,128]{2,1,0:T(8,128)S(1)} all-to-all(f32[8,128,128]{2,1,0:T(8,128)S(1)} %forward.2), channel_id=1, replica_groups=mesh['y'=8,'z_high'=6,'z_low'=2,'narrow'=8] {'narrow'}, dimensions={0} | all-to-all | bytes 1048576 | tf_op jit(solution)/shard_map/all_to_all | solution.py:199
  33.3 12.8 %all_to_all.56.data_ref = f32[8,128,128]{2,1,0:T(8,128)S(1)} all-to-all(f32[8,128,128]{2,1,0:T(8,128)S(1)} %sum_copies.6), channel_id=1, replica_groups=mesh['y'=8,'z_high'=6,'z_low'=2,'narrow'=8] {'narrow'}, dimensions={0} | all-to-all | bytes 1048576 | tf_op jit(solution)/shard_map/all_to_all | solution.py:199
  46.1 0.0 copy-done.1
  46.1 0.0 copy-done.5
  46.2 0.0 copy-done.7
  46.2 0.0 copy-done.9
  46.2 3.6 %backward.2 = f32[16,104,128]{2,1,0:T(8,128)S(1)} custom-call(s32[128]{0:T(128)S(1)} %copy-done.7, s32[128]{0:T(128)S(1)} %copy-done.9, s32[1]{0:T(128)S(6)} %copy.9.used_ref, f32[8,128,128]{2,1,0:T(8,128)S(1)} %all_to_all.56.data_ref, s32[16,1,128]{2,1,0:T(1,128)S(1)} %bitcast.5, bf16[128,128,128]{2,1,0:T(8,128)(2,1)S(1)} %copy-done.1), custom_call_target="tpu_custom_call" | custom-call | tf_op jit(solution)/shard_map/backward/pallas_call | solution.py:166
  49.8 0.0 copy-start.4
  49.8 25.1 %all_to_all.57.got_ref = f32[16,104,128]{2,1,0:T(8,128)S(1)} all-to-all(f32[16,104,128]{2,1,0:T(8,128)S(1)} %backward.2), channel_id=1, replica_groups=mesh['y'=8,'z_high'=6,'z_low'=2,'narrow'=8] {'y','z_low'}, dimensions={0} | all-to-all | bytes 1703936 | tf_op jit(solution)/shard_map/all_to_all | solution.py:199
  74.9 0.1 sum_copies.7
  75.0 24.8 %all_to_all.58.got_ref = f32[6,104,128]{2,1,0:T(8,128)S(1)} all-to-all(f32[6,104,128]{2,1,0:T(8,128)S(1)} %sum_copies.7), channel_id=1, replica_groups=mesh['y'=8,'z_high'=6,'z_low'=2,'narrow'=8] {'z_high'}, dimensions={0} | all-to-all | bytes 638976 | tf_op jit(solution)/shard_map/all_to_all | solution.py:199
  99.7 0.1 sum_copies.8
  99.8 30.5 %all_to_all.59.data_ref = f32[16,104,128]{2,1,0:T(8,128)S(1)} all-to-all(f32[16,104,128]{2,1,0:T(8,128)S(1)} %sum_copies.8), channel_id=1, replica_groups=mesh['y'=8,'z_high'=6,'z_low'=2,'narrow'=8] {'y','z_low'}, dimensions={0} | all-to-all | bytes 1703936 | tf_op jit(solution)/shard_map/all_to_all | solution.py:199
  130.3 0.0 copy-done.4
  130.3 8.0 %forward.3 = f32[8,136,128]{2,1,0:T(8,128)S(1)} custom-call(s32[128]{0:T(128)S(1)} %copy-done.9, s32[128]{0:T(128)S(1)} %copy-done.7, s32[1]{0:T(128)S(6)} %copy.9.used_ref, f32[16,104,128]{2,1,0:T(8,128)S(1)} %all_to_all.59.data_ref, s32[24,1,128]{2,1,0:T(1,128)S(1)} %bitcast.3, bf16[128,128,128]{2,1,0:T(8,128)(2,1)S(1)} %copy-done.1), custom_call_target="tpu_custom_call" | custom-call | tf_op jit(solution)/shard_map/forward/pallas_call | solution.py:166
  138.4 14.0 %all_to_all.60.got_ref = f32[8,136,128]{2,1,0:T(8,128)S(1)} all-to-all(f32[8,136,128]{2,1,0:T(8,128)S(1)} %forward.3), channel_id=1, replica_groups=mesh['y'=8,'z_high'=6,'z_low'=2,'narrow'=8] {'narrow'}, dimensions={0} | all-to-all | bytes 1114112 | tf_op jit(solution)/shard_map/all_to_all | solution.py:199
  152.4 13.1 %all_to_all.61.data_ref = f32[8,136,128]{2,1,0:T(8,128)S(1)} all-to-all(f32[8,136,128]{2,1,0:T(8,128)S(1)} %sum_copies.9), channel_id=1, replica_groups=mesh['y'=8,'z_high'=6,'z_low'=2,'narrow'=8] {'narrow'}, dimensions={0} | all-to-all | bytes 1114112 | tf_op jit(solution)/shard_map/all_to_all | solution.py:199
  165.5 6.2 %backward.3 = (f32[16,104,128]{2,1,0:T(8,128)S(1)}, f32[16,64,128]{2,1,0:T(8,128)S(1)}) custom-call(s32[128]{0:T(128)S(1)} %copy-done.7, s32[128]{0:T(128)S(1)} %copy-done.9, s32[1]{0:T(128)S(6)} %copy.9.used_ref, f32[8,136,128]{2,1,0:T(8,128)S(1)} %all_to_all.61.data_ref, s32[16,1,128]{2,1,0:T(1,128)S(1)} %bitcast.6, bf16[128,128,128]{2,1,0:T(8,128)(2,1)S(1)} %copy-done.1), custom_call_target="tpu_custom_call" | custom-call | tf_op jit(solution)/shard_map/backward/pallas_call | solution.py:166
  171.7 26.1 %all_to_all.62.got_ref = f32[16,104,128]{2,1,0:T(8,128)S(1)} all-to-all(f32[16,104,128]{2,1,0:T(8,128)S(1)} %get-tuple-element.8), channel_id=1, replica_groups=mesh['y'=8,'z_high'=6,'z_low'=2,'narrow'=8] {'y','z_low'}, dimensions={0} | all-to-all | bytes 1703936 | tf_op jit(solution)/shard_map/all_to_all | solution.py:199
  197.8 0.1 sum_copies.10
  197.8 16.9 %all_to_all.63.got_ref = f32[6,104,128]{2,1,0:T(8,128)S(1)} all-to-all(f32[6,104,128]{2,1,0:T(8,128)S(1)} %sum_copies.10), channel_id=1, replica_groups=mesh['y'=8,'z_high'=6,'z_low'=2,'narrow'=8] {'z_high'}, dimensions={0} | all-to-all | bytes 638976 | tf_op jit(solution)/shard_map/all_to_all | solution.py:199
  214.8 0.1 sum_copies.11
  214.8 31.2 %all_to_all.64.data_ref = f32[16,104,128]{2,1,0:T(8,128)S(1)} all-to-all(f32[16,104,128]{2,1,0:T(8,128)S(1)} %sum_copies.11), channel_id=1, replica_groups=mesh['y'=8,'z_high'=6,'z_low'=2,'narrow'=8] {'y','z_low'}, dimensions={0} | all-to-all | bytes 1703936 | tf_op jit(solution)/shard_map/all_to_all | solution.py:199
  246.0 4.3 %finish_items.1 = (f32[64,3072]{1,0:T(8,128)S(1)}, f32[8,32,128]{2,1,0:T(8,128)}, f32[64,64]{1,0:T(8,128)S(1)}) custom-call(f32[16,104,128]{2,1,0:T(8,128)S(1)} %all_to_all.64.data_ref, s32[24,1,128]{2,1,0:T(1,128)S(1)} %bitcast.4), custom_call_target="tpu_custom_call" | custom-call | tf_op jit(solution)/shard_map/finish_items/pallas_call | solution.py:181
  250.3 4.8 %all-to-all-start.10 = ((f32[8,32,128]{2,1,0:T(8,128)}), f32[8,32,128]{2,1,0:T(8,128)S(1)}, u32[]{:S(2)}, u32[]{:S(2)}) async-start(f32[8,32,128]{2,1,0:T(8,128)} %get-tuple-element.11), calls=%async_computation.10 | async-start | bytes 262144 | tf_op jit(solution)/shard_map/all_to_all | solution.py:199
  255.1 1.3 finish_users.1
  256.4 4.0 %all-to-all-done.10.grams_ref = f32[8,32,128]{2,1,0:T(8,128)S(1)} async-done(((f32[8,32,128]{2,1,0:T(8,128)}), f32[8,32,128]{2,1,0:T(8,128)S(1)}, u32[]{:S(2)}, u32[]{:S(2)}) %all-to-all-start.10) | async-done | bytes 131104 | tf_op jit(solution)/shard_map/all_to_all | solution.py:199
  260.4 3.5 %finish_vectors.1 = f32[64,3072]{1,0:T(8,128)} custom-call(f32[64,3072]{1,0:T(8,128)S(1)} %get-tuple-element.10.raw_ref, f32[8,32,128]{2,1,0:T(8,128)S(1)} %all-to-all-done.10.grams_ref), custom_call_target="tpu_custom_call" | custom-call | tf_op jit(solution)/shard_map/finish_vectors/pallas_call | solution.py:181
  (2 shorter events, 0.1 us)
Async XLA Ops:
  1.3 2.2 copy-start
  3.5 1.1 copy-start.2
  4.6 0.7 copy-start.3
  5.3 0.7 copy-start.6
  6.0 0.7 copy-start.8
  6.6 39.5 %copy-start.1 = (bf16[128,128,128]{2,1,0:T(8,128)(2,1)S(1)}, bf16[128,128,128]{2,1,0:T(8,128)(2,1)}, u32[]{:S(2)}) copy-start(bf16[128,128,128]{2,1,0:T(8,128)(2,1)} %tiles_ref.7) | copy-start | bytes 12582916
  6.6 39.5 %copy-start.5 = (s32[2048]{0:T(1024)S(1)}, s32[2048]{0:T(1024)}, u32[]{:S(2)}) copy-start(s32[2048]{0:T(1024)} %param.11) | copy-start | bytes 24580
  6.6 39.5 %copy-start.7 = (s32[128]{0:T(128)S(1)}, s32[128]{0:T(128)}, u32[]{:S(2)}) copy-start(s32[128]{0:T(128)} %src_ref.7) | copy-start | bytes 1540
  6.6 39.5 %copy-start.9 = (s32[128]{0:T(128)S(1)}, s32[128]{0:T(128)}, u32[]{:S(2)}) copy-start(s32[128]{0:T(128)} %dst_ref.7) | copy-start | bytes 1540
  49.8 80.5 %copy-start.4 = (s32[3072]{0:T(1024)S(1)}, s32[3072]{0:T(1024)}, u32[]{:S(2)}) copy-start(s32[3072]{0:T(1024)} %param.12) | copy-start | bytes 36868
  250.3 10.1 %all-to-all-start.10 = ((f32[8,32,128]{2,1,0:T(8,128)}), f32[8,32,128]{2,1,0:T(8,128)S(1)}, u32[]{:S(2)}, u32[]{:S(2)}) async-start(f32[8,32,128]{2,1,0:T(8,128)} %get-tuple-element.11), calls=%async_computation.10 | async-start | bytes 262144 | tf_op jit(solution)/shard_map/all_to_all | solution.py:199

commit v5 on v4

--- a/solution.py
+++ b/solution.py
@@ -14,6 +14,7 @@
 SUB = 8
 WIDTH = 4
 VMEM_LIMIT = 16 * 1024 * 1024
+BEGIN_LIMIT = 57 * 1024 * 1024
 FULL = lax.Precision.HIGHEST
 VMEM = pl.BlockSpec(memory_space=pltpu.VMEM)
 SMEM = pl.BlockSpec(memory_space=pltpu.SMEM)
@@ -109,10 +110,30 @@
     dims = (((1,), (1,)), ((), ())) if forward else (((1,), (0,)), ((), ()))
 
     def body(src_ref, dst_ref, used_ref, data_ref, degree_ref, tiles_ref, out_ref, *rest):
-        if keep_raw:
+        if begins:
+            x_ref, sums_ref, data_here, degree_here, tiles_here, whole_sem, group_sem = rest
+
+            def group_copy(step):
+                rows = pl.ds(step * GROUP, GROUP)
+                return pltpu.make_async_copy(tiles_ref.at[rows], tiles_here.at[rows], group_sem.at[step])
+
+            copies = [
+                pltpu.make_async_copy(degree_ref, degree_here, whole_sem.at[0]),
+                pltpu.make_async_copy(data_ref, data_here, whole_sem.at[1]),
+            ]
+            for copy in copies + [group_copy(step) for step in range(slots // GROUP)]:
+                copy.start()
+            for copy in copies:
+                copy.wait()
+            product_phase(src_ref, dst_ref, used_ref, data_here, degree_here, tiles_here, out_ref, None, x_ref, sums_ref, group_copy)
+        elif keep_raw:
             raw_ref, x_ref, sums_ref = rest
+            product_phase(src_ref, dst_ref, used_ref, data_ref, degree_ref, tiles_ref, out_ref, raw_ref, x_ref, sums_ref, None)
         else:
             x_ref, sums_ref = rest
+            product_phase(src_ref, dst_ref, used_ref, data_ref, degree_ref, tiles_ref, out_ref, None, x_ref, sums_ref, None)
+
+    def product_phase(src_ref, dst_ref, used_ref, data_ref, degree_ref, tiles_ref, out_ref, raw_ref, x_ref, sums_ref, copy_of):
         sums_ref[...] = jnp.zeros_like(sums_ref)
         if have_gram:
             inverse = inverse_factor(gram_panels(data_ref, per_chunk, vectors, gram_count))
@@ -148,6 +169,8 @@
 
         @pl.loop(0, slots // GROUP)
         def _(step):
+            if copy_of is not None:
+                copy_of(step).wait()
             for slot in range(GROUP):
                 at = step * GROUP + slot
                 product = lax.dot_general(
@@ -163,14 +186,36 @@
     out_shape = [jax.ShapeDtypeStruct((out_chunks, out_rows, tile), jnp.float32)]
     if keep_raw:
         out_shape.append(jax.ShapeDtypeStruct((blocks, vectors, tile), jnp.float32))
+    scratch = [
+        pltpu.VMEM((blocks, terms * vectors, tile), jnp.bfloat16),
+        pltpu.VMEM((blocks_out + 1, vectors, tile), jnp.float32),
+    ]
+    if begins:
+        scratch += [
+            pltpu.VMEM(data.shape, data.dtype),
+            pltpu.VMEM(degree.shape, degree.dtype),
+            pltpu.VMEM(tiles.shape, tiles.dtype),
+            pltpu.SemaphoreType.DMA((2,)),
+            pltpu.SemaphoreType.DMA((slots // GROUP,)),
+        ]
+        return pl.pallas_call(
+            body,
+            grid_spec=pltpu.PrefetchScalarGridSpec(
+                num_scalar_prefetch=3,
+                grid=(1,),
+                in_specs=[pl.BlockSpec(memory_space=pl.ANY)] * 3,
+                out_specs=[VMEM],
+                scratch_shapes=scratch,
+            ),
+            out_shape=out_shape,
+            compiler_params=pltpu.CompilerParams(vmem_limit_bytes=BEGIN_LIMIT),
+            name="forward_begin",
+        )(src, dst, used, data, degree, tiles)
     return pl.pallas_call(
         body,
         in_specs=[SMEM] * 3 + [VMEM] * 3,
         out_specs=[VMEM] * len(out_shape),
-        scratch_shapes=[
-            pltpu.VMEM((blocks, terms * vectors, tile), jnp.bfloat16),
-            pltpu.VMEM((blocks_out + 1, vectors, tile), jnp.float32),
-        ],
+        scratch_shapes=scratch,
         out_shape=out_shape,
         compiler_params=pltpu.CompilerParams(vmem_limit_bytes=VMEM_LIMIT),
         name="forward" if forward else "backward",

time: 265 us -> 263 us (level)
  local copies, waits for them, and re-layouts: 5.35 us -> 0.02 us
  Pallas kernels: 31.7 us -> 35.5 us
    pallas_call x0 -> x1, Pallas kernels: none -> 8.2 us  [phase(): pl.pallas_call(body, grid_spec=pltpu.PrefetchScalarGridSpec(num_scalar_pr...]
    unnamed x20 -> x10, local copies, waits for them, and re-layouts: 5.35 us -> 0.02 us
    pallas_call x4 -> x3, Pallas kernels: 22.3 us -> 17.9 us  [phase(): pl.pallas_call(body, in_specs=[SMEM] * 3 + [VMEM] * 3, out_specs=[VMEM] *...]
where the time goes in v5:
time: 263 us
  blocking collectives  217 us (83%)
  Pallas kernels  35.5 us (13%)
  starting transfers between devices  4.77 us (2%)
  waiting for transfers between devices  3.95 us (2%)
    all_to_all x10, blocking collectives, exchange(): return lax.all_to_all(data, axis, 0, 0)  217 us
    pallas_call x3, Pallas kernels, phase(): pl.pallas_call(body, in_specs=[SMEM] * 3 + [VMEM] * 3, out_specs=[VMEM] *...  17.9 us
    pallas_call x9, Pallas kernels, call(): pl.pallas_call(body, in_specs=[VMEM] * len(inputs), out_specs=[VMEM] * le...  9.41 us
    pallas_call x1, Pallas kernels, phase(): pl.pallas_call(body, grid_spec=pltpu.PrefetchScalarGridSpec(num_scalar_pr...  8.2 us
  transfers between devices with their start and end apart: 1, of which 1 were waited for; matrix products, arithmetic and copies ran while one was open for 0% of the time, Pallas kernels for 1%

profile of v5, /device:TPU:1, one launch (start us, length us, event | category | flops | bytes accessed | tf_op | source)
XLA Modules:
  0.0 262.5 jit_solution(12986983400836115660)
XLA Ops:
  1.3 0.0 copy-start
  1.3 0.0 copy-start.2
  1.3 0.0 copy-start.3
  1.3 0.0 copy-start.4
  1.3 8.2 %forward_begin.1 = f32[8,128,128]{2,1,0:T(8,128)} custom-call(s32[128]{0:T(128)} %dst_ref.7, s32[128]{0:T(128)} %src_ref.7, s32[1]{0:T(128)S(6)} %copy.9.used_ref, f32[64,3072]{1,0:T(8,128)} %data_ref.1, s32[24,1,128]{2,1,0:T(1,128)} %bitcast.2, bf16[128,128,128]{2,1,0:T(8,128)(2,1)} %tiles_ref.7), custom_call_target="tpu_custom_call" | custom-call | tf_op jit(solution)/shard_map/forward_begin/pallas_call | solution.py:201
  9.5 23.3 %all_to_all.55.got_ref = f32[8,128,128]{2,1,0:T(8,128)S(1)} all-to-all(f32[8,128,128]{2,1,0:T(8,128)} %forward_begin.1), channel_id=1, replica_groups=mesh['y'=8,'z_high'=6,'z_low'=2,'narrow'=8] {'narrow'}, dimensions={0} | all-to-all | bytes 1048576 | tf_op jit(solution)/shard_map/all_to_all | solution.py:244
  32.8 12.8 %all_to_all.56.data_ref = f32[8,128,128]{2,1,0:T(8,128)S(1)} all-to-all(f32[8,128,128]{2,1,0:T(8,128)S(1)} %sum_copies.6), channel_id=1, replica_groups=mesh['y'=8,'z_high'=6,'z_low'=2,'narrow'=8] {'narrow'}, dimensions={0} | all-to-all | bytes 1048576 | tf_op jit(solution)/shard_map/all_to_all | solution.py:244
  45.7 0.0 copy-done
  45.7 0.0 copy-done.2
  45.7 0.0 copy-done.3
  45.7 0.0 copy-done.4
  45.7 3.6 %backward.2 = f32[16,104,128]{2,1,0:T(8,128)S(1)} custom-call(s32[128]{0:T(128)S(1)} %copy-done.3, s32[128]{0:T(128)S(1)} %copy-done.4, s32[1]{0:T(128)S(6)} %copy.9.used_ref, f32[8,128,128]{2,1,0:T(8,128)S(1)} %all_to_all.56.data_ref, s32[16,1,128]{2,1,0:T(1,128)S(1)} %bitcast.5, bf16[128,128,128]{2,1,0:T(8,128)(2,1)S(1)} %copy-done), custom_call_target="tpu_custom_call" | custom-call | tf_op jit(solution)/shard_map/backward/pallas_call | solution.py:214
  49.3 0.0 copy-start.1
  49.3 25.1 %all_to_all.57.got_ref = f32[16,104,128]{2,1,0:T(8,128)S(1)} all-to-all(f32[16,104,128]{2,1,0:T(8,128)S(1)} %backward.2), channel_id=1, replica_groups=mesh['y'=8,'z_high'=6,'z_low'=2,'narrow'=8] {'y','z_low'}, dimensions={0} | all-to-all | bytes 1703936 | tf_op jit(solution)/shard_map/all_to_all | solution.py:244
  74.4 0.1 sum_copies.7
  74.5 24.0 %all_to_all.58.got_ref = f32[6,104,128]{2,1,0:T(8,128)S(1)} all-to-all(f32[6,104,128]{2,1,0:T(8,128)S(1)} %sum_copies.7), channel_id=1, replica_groups=mesh['y'=8,'z_high'=6,'z_low'=2,'narrow'=8] {'z_high'}, dimensions={0} | all-to-all | bytes 638976 | tf_op jit(solution)/shard_map/all_to_all | solution.py:244
  98.4 0.1 sum_copies.8
  98.5 30.5 %all_to_all.59.data_ref = f32[16,104,128]{2,1,0:T(8,128)S(1)} all-to-all(f32[16,104,128]{2,1,0:T(8,128)S(1)} %sum_copies.8), channel_id=1, replica_groups=mesh['y'=8,'z_high'=6,'z_low'=2,'narrow'=8] {'y','z_low'}, dimensions={0} | all-to-all | bytes 1703936 | tf_op jit(solution)/shard_map/all_to_all | solution.py:244
  129.0 0.0 copy-done.1
  129.0 8.0 %forward.1 = f32[8,136,128]{2,1,0:T(8,128)S(1)} custom-call(s32[128]{0:T(128)S(1)} %copy-done.4, s32[128]{0:T(128)S(1)} %copy-done.3, s32[1]{0:T(128)S(6)} %copy.9.used_ref, f32[16,104,128]{2,1,0:T(8,128)S(1)} %all_to_all.59.data_ref, s32[24,1,128]{2,1,0:T(1,128)S(1)} %bitcast.3, bf16[128,128,128]{2,1,0:T(8,128)(2,1)S(1)} %copy-done), custom_call_target="tpu_custom_call" | custom-call | tf_op jit(solution)/shard_map/forward/pallas_call | solution.py:214
  137.0 14.0 %all_to_all.60.got_ref = f32[8,136,128]{2,1,0:T(8,128)S(1)} all-to-all(f32[8,136,128]{2,1,0:T(8,128)S(1)} %forward.1), channel_id=1, replica_groups=mesh['y'=8,'z_high'=6,'z_low'=2,'narrow'=8] {'narrow'}, dimensions={0} | all-to-all | bytes 1114112 | tf_op jit(solution)/shard_map/all_to_all | solution.py:244
  151.1 13.1 %all_to_all.61.data_ref = f32[8,136,128]{2,1,0:T(8,128)S(1)} all-to-all(f32[8,136,128]{2,1,0:T(8,128)S(1)} %sum_copies.9), channel_id=1, replica_groups=mesh['y'=8,'z_high'=6,'z_low'=2,'narrow'=8] {'narrow'}, dimensions={0} | all-to-all | bytes 1114112 | tf_op jit(solution)/shard_map/all_to_all | solution.py:244
  164.2 6.2 %backward.3 = (f32[16,104,128]{2,1,0:T(8,128)S(1)}, f32[16,64,128]{2,1,0:T(8,128)S(1)}) custom-call(s32[128]{0:T(128)S(1)} %copy-done.3, s32[128]{0:T(128)S(1)} %copy-done.4, s32[1]{0:T(128)S(6)} %copy.9.used_ref, f32[8,136,128]{2,1,0:T(8,128)S(1)} %all_to_all.61.data_ref, s32[16,1,128]{2,1,0:T(1,128)S(1)} %bitcast.6, bf16[128,128,128]{2,1,0:T(8,128)(2,1)S(1)} %copy-done), custom_call_target="tpu_custom_call" | custom-call | tf_op jit(solution)/shard_map/backward/pallas_call | solution.py:214
  170.4 26.1 %all_to_all.62.got_ref = f32[16,104,128]{2,1,0:T(8,128)S(1)} all-to-all(f32[16,104,128]{2,1,0:T(8,128)S(1)} %get-tuple-element.8), channel_id=1, replica_groups=mesh['y'=8,'z_high'=6,'z_low'=2,'narrow'=8] {'y','z_low'}, dimensions={0} | all-to-all | bytes 1703936 | tf_op jit(solution)/shard_map/all_to_all | solution.py:244
  196.5 0.1 sum_copies.10
  196.5 16.9 %all_to_all.63.got_ref = f32[6,104,128]{2,1,0:T(8,128)S(1)} all-to-all(f32[6,104,128]{2,1,0:T(8,128)S(1)} %sum_copies.10), channel_id=1, replica_groups=mesh['y'=8,'z_high'=6,'z_low'=2,'narrow'=8] {'z_high'}, dimensions={0} | all-to-all | bytes 638976 | tf_op jit(solution)/shard_map/all_to_all | solution.py:244
  213.5 0.1 sum_copies.11
  213.5 31.2 %all_to_all.64.data_ref = f32[16,104,128]{2,1,0:T(8,128)S(1)} all-to-all(f32[16,104,128]{2,1,0:T(8,128)S(1)} %sum_copies.11), channel_id=1, replica_groups=mesh['y'=8,'z_high'=6,'z_low'=2,'narrow'=8] {'y','z_low'}, dimensions={0} | all-to-all | bytes 1703936 | tf_op jit(solution)/shard_map/all_to_all | solution.py:244
  244.7 4.3 %finish_items.1 = (f32[64,3072]{1,0:T(8,128)S(1)}, f32[8,32,128]{2,1,0:T(8,128)}, f32[64,64]{1,0:T(8,128)S(1)}) custom-call(f32[16,104,128]{2,1,0:T(8,128)S(1)} %all_to_all.64.data_ref, s32[24,1,128]{2,1,0:T(1,128)S(1)} %bitcast.4), custom_call_target="tpu_custom_call" | custom-call | tf_op jit(solution)/shard_map/finish_items/pallas_call | solution.py:226
  249.0 4.8 %all-to-all-start.10 = ((f32[8,32,128]{2,1,0:T(8,128)}), f32[8,32,128]{2,1,0:T(8,128)S(1)}, u32[]{:S(2)}, u32[]{:S(2)}) async-start(f32[8,32,128]{2,1,0:T(8,128)} %get-tuple-element.11), calls=%async_computation.10 | async-start | bytes 262144 | tf_op jit(solution)/shard_map/all_to_all | solution.py:244
  253.8 1.3 finish_users.1
  255.1 4.0 %all-to-all-done.10.grams_ref = f32[8,32,128]{2,1,0:T(8,128)S(1)} async-done(((f32[8,32,128]{2,1,0:T(8,128)}), f32[8,32,128]{2,1,0:T(8,128)S(1)}, u32[]{:S(2)}, u32[]{:S(2)}) %all-to-all-start.10) | async-done | bytes 131104 | tf_op jit(solution)/shard_map/all_to_all | solution.py:244
  259.1 3.4 %finish_vectors.1 = f32[64,3072]{1,0:T(8,128)} custom-call(f32[64,3072]{1,0:T(8,128)S(1)} %get-tuple-element.10.raw_ref, f32[8,32,128]{2,1,0:T(8,128)S(1)} %all-to-all-done.10.grams_ref), custom_call_target="tpu_custom_call" | custom-call | tf_op jit(solution)/shard_map/finish_vectors/pallas_call | solution.py:226
  (2 shorter events, 0.1 us)
Async XLA Ops:
  1.3 44.4 %copy-start = (bf16[128,128,128]{2,1,0:T(8,128)(2,1)S(1)}, bf16[128,128,128]{2,1,0:T(8,128)(2,1)}, u32[]{:S(2)}) copy-start(bf16[128,128,128]{2,1,0:T(8,128)(2,1)} %tiles_ref.7) | copy-start | bytes 12582916
  1.3 44.4 %copy-start.2 = (s32[2048]{0:T(1024)S(1)}, s32[2048]{0:T(1024)}, u32[]{:S(2)}) copy-start(s32[2048]{0:T(1024)} %param.11) | copy-start | bytes 24580
  1.3 44.4 %copy-start.3 = (s32[128]{0:T(128)S(1)}, s32[128]{0:T(128)}, u32[]{:S(2)}) copy-start(s32[128]{0:T(128)} %src_ref.7) | copy-start | bytes 1540
  1.3 44.4 %copy-start.4 = (s32[128]{0:T(128)S(1)}, s32[128]{0:T(128)}, u32[]{:S(2)}) copy-start(s32[128]{0:T(128)} %dst_ref.7) | copy-start | bytes 1540
  49.3 79.7 %copy-start.1 = (s32[3072]{0:T(1024)S(1)}, s32[3072]{0:T(1024)}, u32[]{:S(2)}) copy-start(s32[3072]{0:T(1024)} %param.12) | copy-start | bytes 36868
  249.0 10.1 %all-to-all-start.10 = ((f32[8,32,128]{2,1,0:T(8,128)}), f32[8,32,128]{2,1,0:T(8,128)S(1)}, u32[]{:S(2)}, u32[]{:S(2)}) async-start(f32[8,32,128]{2,1,0:T(8,128)} %get-tuple-element.11), calls=%async_computation.10 | async-start | bytes 262144 | tf_op jit(solution)/shard_map/all_to_all | solution.py:244

commit v6 on v5

--- a/solution.py
+++ b/solution.py
@@ -8,7 +8,8 @@
 from jax.sharding import Mesh, PartitionSpec as P
 
 ITERS = 2
-GROUP = 16
+GROUP = 64
+BEGIN_GROUP = 32
 Y_CHIPS = 8
 Z_PAIR = 2
 SUB = 8
@@ -107,6 +108,7 @@
     terms = 1 if begins else 2
     out_per = blocks_out * vectors // out_chunks
     out_rows = out_per + (SUB if send_gram else 0)
+    group_slots = BEGIN_GROUP if begins else GROUP
     dims = (((1,), (1,)), ((), ())) if forward else (((1,), (0,)), ((), ()))
 
     def body(src_ref, dst_ref, used_ref, data_ref, degree_ref, tiles_ref, out_ref, *rest):
@@ -114,14 +116,14 @@
             x_ref, sums_ref, data_here, degree_here, tiles_here, whole_sem, group_sem = rest
 
             def group_copy(step):
-                rows = pl.ds(step * GROUP, GROUP)
+                rows = pl.ds(step * group_slots, group_slots)
                 return pltpu.make_async_copy(tiles_ref.at[rows], tiles_here.at[rows], group_sem.at[step])
 
             copies = [
                 pltpu.make_async_copy(degree_ref, degree_here, whole_sem.at[0]),
                 pltpu.make_async_copy(data_ref, data_here, whole_sem.at[1]),
             ]
-            for copy in copies + [group_copy(step) for step in range(slots // GROUP)]:
+            for copy in copies + [group_copy(step) for step in range(slots // group_slots)]:
                 copy.start()
             for copy in copies:
                 copy.wait()
@@ -167,12 +169,12 @@
                 inside = c * SUB < vectors
                 out_ref[c, out_per:, :] = both[c * SUB : (c + 1) * SUB] if inside else jnp.zeros((SUB, tile), jnp.float32)
 
-        @pl.loop(0, slots // GROUP)
+        @pl.loop(0, slots // group_slots)
         def _(step):
             if copy_of is not None:
                 copy_of(step).wait()
-            for slot in range(GROUP):
-                at = step * GROUP + slot
+            for slot in range(group_slots):
+                at = step * group_slots + slot
                 product = lax.dot_general(
                     x_ref[src_ref[at]], tiles_ref[at], dims, preferred_element_type=jnp.float32
                 )
@@ -196,7 +198,7 @@
             pltpu.VMEM(degree.shape, degree.dtype),
             pltpu.VMEM(tiles.shape, tiles.dtype),
             pltpu.SemaphoreType.DMA((2,)),
-            pltpu.SemaphoreType.DMA((slots // GROUP,)),
+            pltpu.SemaphoreType.DMA((slots // group_slots,)),
         ]
         return pl.pallas_call(
             body,

time: 263 us -> 260 us (0.989)
  Pallas kernels: 35.5 us -> 32.2 us
    pallas_call x3, Pallas kernels: 17.9 us -> 15.2 us  [phase(): pl.pallas_call(body, in_specs=[SMEM] * 3 + [VMEM] * 3, out_specs=[VMEM] *...]
where the time goes in v6:
time: 260 us; the launch traced here: 259 us
  blocking collectives  217 us (83%)
  Pallas kernels  32.2 us (12%)
  starting transfers between devices  4.77 us (2%)
  waiting for transfers between devices  3.95 us (2%)
    all_to_all x10, blocking collectives, exchange(): return lax.all_to_all(data, axis, 0, 0)  217 us
    pallas_call x3, Pallas kernels, phase(): pl.pallas_call(body, in_specs=[SMEM] * 3 + [VMEM] * 3, out_specs=[VMEM] *...  15.2 us
    pallas_call x9, Pallas kernels, call(): pl.pallas_call(body, in_specs=[VMEM] * len(inputs), out_specs=[VMEM] * le...  9.4 us
    pallas_call x1, Pallas kernels, phase(): pl.pallas_call(body, grid_spec=pltpu.PrefetchScalarGridSpec(num_scalar_pr...  7.59 us
  transfers between devices with their start and end apart: 1, of which 1 were waited for; matrix products, arithmetic and copies ran while one was open for 0% of the time, Pallas kernels for 1%

profile of v6, /device:TPU:1, one launch (start us, length us, event | category | flops | bytes accessed | tf_op | source)
XLA Modules:
  0.0 259.2 jit_solution(18437576282453417973)
XLA Ops:
  1.3 0.0 copy-start
  1.3 0.0 copy-start.2
  1.3 0.0 copy-start.3
  1.3 0.0 copy-start.4
  1.3 7.6 %forward_begin.1 = f32[8,128,128]{2,1,0:T(8,128)} custom-call(s32[128]{0:T(128)} %dst_ref.7, s32[128]{0:T(128)} %src_ref.7, s32[1]{0:T(128)S(6)} %copy.9.used_ref, f32[64,3072]{1,0:T(8,128)} %data_ref.1, s32[24,1,128]{2,1,0:T(1,128)} %bitcast.2, bf16[128,128,128]{2,1,0:T(8,128)(2,1)} %tiles_ref.7), custom_call_target="tpu_custom_call" | custom-call | tf_op jit(solution)/shard_map/forward_begin/pallas_call | solution.py:203
  8.9 23.3 %all_to_all.55.got_ref = f32[8,128,128]{2,1,0:T(8,128)S(1)} all-to-all(f32[8,128,128]{2,1,0:T(8,128)} %forward_begin.1), channel_id=1, replica_groups=mesh['y'=8,'z_high'=6,'z_low'=2,'narrow'=8] {'narrow'}, dimensions={0} | all-to-all | bytes 1048576 | tf_op jit(solution)/shard_map/all_to_all | solution.py:246
  32.2 12.8 %all_to_all.56.data_ref = f32[8,128,128]{2,1,0:T(8,128)S(1)} all-to-all(f32[8,128,128]{2,1,0:T(8,128)S(1)} %sum_copies.6), channel_id=1, replica_groups=mesh['y'=8,'z_high'=6,'z_low'=2,'narrow'=8] {'narrow'}, dimensions={0} | all-to-all | bytes 1048576 | tf_op jit(solution)/shard_map/all_to_all | solution.py:246
  45.0 0.0 copy-done
  45.0 0.0 copy-done.2
  45.0 0.0 copy-done.3
  45.0 0.0 copy-done.4
  45.1 2.7 %backward.2 = f32[16,104,128]{2,1,0:T(8,128)S(1)} custom-call(s32[128]{0:T(128)S(1)} %copy-done.3, s32[128]{0:T(128)S(1)} %copy-done.4, s32[1]{0:T(128)S(6)} %copy.9.used_ref, f32[8,128,128]{2,1,0:T(8,128)S(1)} %all_to_all.56.data_ref, s32[16,1,128]{2,1,0:T(1,128)S(1)} %bitcast.5, bf16[128,128,128]{2,1,0:T(8,128)(2,1)S(1)} %copy-done), custom_call_target="tpu_custom_call" | custom-call | tf_op jit(solution)/shard_map/backward/pallas_call | solution.py:216
  47.8 0.0 copy-start.1
  47.8 25.1 %all_to_all.57.got_ref = f32[16,104,128]{2,1,0:T(8,128)S(1)} all-to-all(f32[16,104,128]{2,1,0:T(8,128)S(1)} %backward.2), channel_id=1, replica_groups=mesh['y'=8,'z_high'=6,'z_low'=2,'narrow'=8] {'y','z_low'}, dimensions={0} | all-to-all | bytes 1703936 | tf_op jit(solution)/shard_map/all_to_all | solution.py:246
  72.8 0.1 sum_copies.7
  72.9 24.0 %all_to_all.58.got_ref = f32[6,104,128]{2,1,0:T(8,128)S(1)} all-to-all(f32[6,104,128]{2,1,0:T(8,128)S(1)} %sum_copies.7), channel_id=1, replica_groups=mesh['y'=8,'z_high'=6,'z_low'=2,'narrow'=8] {'z_high'}, dimensions={0} | all-to-all | bytes 638976 | tf_op jit(solution)/shard_map/all_to_all | solution.py:246
  96.8 0.1 sum_copies.8
  96.9 30.5 %all_to_all.59.data_ref = f32[16,104,128]{2,1,0:T(8,128)S(1)} all-to-all(f32[16,104,128]{2,1,0:T(8,128)S(1)} %sum_copies.8), channel_id=1, replica_groups=mesh['y'=8,'z_high'=6,'z_low'=2,'narrow'=8] {'y','z_low'}, dimensions={0} | all-to-all | bytes 1703936 | tf_op jit(solution)/shard_map/all_to_all | solution.py:246
  127.4 0.0 copy-done.1
  127.4 7.3 %forward.1 = f32[8,136,128]{2,1,0:T(8,128)S(1)} custom-call(s32[128]{0:T(128)S(1)} %copy-done.4, s32[128]{0:T(128)S(1)} %copy-done.3, s32[1]{0:T(128)S(6)} %copy.9.used_ref, f32[16,104,128]{2,1,0:T(8,128)S(1)} %all_to_all.59.data_ref, s32[24,1,128]{2,1,0:T(1,128)S(1)} %bitcast.3, bf16[128,128,128]{2,1,0:T(8,128)(2,1)S(1)} %copy-done), custom_call_target="tpu_custom_call" | custom-call | tf_op jit(solution)/shard_map/forward/pallas_call | solution.py:216
  134.7 14.0 %all_to_all.60.got_ref = f32[8,136,128]{2,1,0:T(8,128)S(1)} all-to-all(f32[8,136,128]{2,1,0:T(8,128)S(1)} %forward.1), channel_id=1, replica_groups=mesh['y'=8,'z_high'=6,'z_low'=2,'narrow'=8] {'narrow'}, dimensions={0} | all-to-all | bytes 1114112 | tf_op jit(solution)/shard_map/all_to_all | solution.py:246
  148.8 13.1 %all_to_all.61.data_ref = f32[8,136,128]{2,1,0:T(8,128)S(1)} all-to-all(f32[8,136,128]{2,1,0:T(8,128)S(1)} %sum_copies.9), channel_id=1, replica_groups=mesh['y'=8,'z_high'=6,'z_low'=2,'narrow'=8] {'narrow'}, dimensions={0} | all-to-all | bytes 1114112 | tf_op jit(solution)/shard_map/all_to_all | solution.py:246
  161.9 5.2 %backward.3 = (f32[16,104,128]{2,1,0:T(8,128)S(1)}, f32[16,64,128]{2,1,0:T(8,128)S(1)}) custom-call(s32[128]{0:T(128)S(1)} %copy-done.3, s32[128]{0:T(128)S(1)} %copy-done.4, s32[1]{0:T(128)S(6)} %copy.9.used_ref, f32[8,136,128]{2,1,0:T(8,128)S(1)} %all_to_all.61.data_ref, s32[16,1,128]{2,1,0:T(1,128)S(1)} %bitcast.6, bf16[128,128,128]{2,1,0:T(8,128)(2,1)S(1)} %copy-done), custom_call_target="tpu_custom_call" | custom-call | tf_op jit(solution)/shard_map/backward/pallas_call | solution.py:216
  167.1 26.1 %all_to_all.62.got_ref = f32[16,104,128]{2,1,0:T(8,128)S(1)} all-to-all(f32[16,104,128]{2,1,0:T(8,128)S(1)} %get-tuple-element.8), channel_id=1, replica_groups=mesh['y'=8,'z_high'=6,'z_low'=2,'narrow'=8] {'y','z_low'}, dimensions={0} | all-to-all | bytes 1703936 | tf_op jit(solution)/shard_map/all_to_all | solution.py:246
  193.2 0.1 sum_copies.10
  193.2 16.9 %all_to_all.63.got_ref = f32[6,104,128]{2,1,0:T(8,128)S(1)} all-to-all(f32[6,104,128]{2,1,0:T(8,128)S(1)} %sum_copies.10), channel_id=1, replica_groups=mesh['y'=8,'z_high'=6,'z_low'=2,'narrow'=8] {'z_high'}, dimensions={0} | all-to-all | bytes 638976 | tf_op jit(solution)/shard_map/all_to_all | solution.py:246
  210.1 0.1 sum_copies.11
  210.2 31.2 %all_to_all.64.data_ref = f32[16,104,128]{2,1,0:T(8,128)S(1)} all-to-all(f32[16,104,128]{2,1,0:T(8,128)S(1)} %sum_copies.11), channel_id=1, replica_groups=mesh['y'=8,'z_high'=6,'z_low'=2,'narrow'=8] {'y','z_low'}, dimensions={0} | all-to-all | bytes 1703936 | tf_op jit(solution)/shard_map/all_to_all | solution.py:246
  241.4 4.3 %finish_items.1 = (f32[64,3072]{1,0:T(8,128)S(1)}, f32[8,32,128]{2,1,0:T(8,128)}, f32[64,64]{1,0:T(8,128)S(1)}) custom-call(f32[16,104,128]{2,1,0:T(8,128)S(1)} %all_to_all.64.data_ref, s32[24,1,128]{2,1,0:T(1,128)S(1)} %bitcast.4), custom_call_target="tpu_custom_call" | custom-call | tf_op jit(solution)/shard_map/finish_items/pallas_call | solution.py:228
  245.7 4.8 %all-to-all-start.10 = ((f32[8,32,128]{2,1,0:T(8,128)}), f32[8,32,128]{2,1,0:T(8,128)S(1)}, u32[]{:S(2)}, u32[]{:S(2)}) async-start(f32[8,32,128]{2,1,0:T(8,128)} %get-tuple-element.11), calls=%async_computation.10 | async-start | bytes 262144 | tf_op jit(solution)/shard_map/all_to_all | solution.py:246
  250.5 1.3 finish_users.1
  251.8 4.0 %all-to-all-done.10.grams_ref = f32[8,32,128]{2,1,0:T(8,128)S(1)} async-done(((f32[8,32,128]{2,1,0:T(8,128)}), f32[8,32,128]{2,1,0:T(8,128)S(1)}, u32[]{:S(2)}, u32[]{:S(2)}) %all-to-all-start.10) | async-done | bytes 131104 | tf_op jit(solution)/shard_map/all_to_all | solution.py:246
  255.8 3.4 %finish_vectors.1 = f32[64,3072]{1,0:T(8,128)} custom-call(f32[64,3072]{1,0:T(8,128)S(1)} %get-tuple-element.10.raw_ref, f32[8,32,128]{2,1,0:T(8,128)S(1)} %all-to-all-done.10.grams_ref), custom_call_target="tpu_custom_call" | custom-call | tf_op jit(solution)/shard_map/finish_vectors/pallas_call | solution.py:228
  (2 shorter events, 0.1 us)
Async XLA Ops:
  1.3 43.8 %copy-start = (bf16[128,128,128]{2,1,0:T(8,128)(2,1)S(1)}, bf16[128,128,128]{2,1,0:T(8,128)(2,1)}, u32[]{:S(2)}) copy-start(bf16[128,128,128]{2,1,0:T(8,128)(2,1)} %tiles_ref.7) | copy-start | bytes 12582916
  1.3 43.8 %copy-start.2 = (s32[2048]{0:T(1024)S(1)}, s32[2048]{0:T(1024)}, u32[]{:S(2)}) copy-start(s32[2048]{0:T(1024)} %param.11) | copy-start | bytes 24580
  1.3 43.7 %copy-start.3 = (s32[128]{0:T(128)S(1)}, s32[128]{0:T(128)}, u32[]{:S(2)}) copy-start(s32[128]{0:T(128)} %src_ref.7) | copy-start | bytes 1540
  1.3 43.7 %copy-start.4 = (s32[128]{0:T(128)S(1)}, s32[128]{0:T(128)}, u32[]{:S(2)}) copy-start(s32[128]{0:T(128)} %dst_ref.7) | copy-start | bytes 1540
  47.8 79.7 %copy-start.1 = (s32[3072]{0:T(1024)S(1)}, s32[3072]{0:T(1024)}, u32[]{:S(2)}) copy-start(s32[3072]{0:T(1024)} %param.12) | copy-start | bytes 36868
  245.7 10.1 %all-to-all-start.10 = ((f32[8,32,128]{2,1,0:T(8,128)}), f32[8,32,128]{2,1,0:T(8,128)S(1)}, u32[]{:S(2)}, u32[]{:S(2)}) async-start(f32[8,32,128]{2,1,0:T(8,128)} %get-tuple-element.11), calls=%async_computation.10 | async-start | bytes 262144 | tf_op jit(solution)/shard_map/all_to_all | solution.py:246

commit v7 on v6

--- a/solution.py
+++ b/solution.py
@@ -68,46 +68,58 @@
     return jnp.concatenate(rows, axis=0)[:, vectors:]
 
 
-def padded(gram):
-    return jnp.concatenate([gram, jnp.zeros_like(gram)], axis=1)
-
-
-def read_block(ref, block, vectors, per_chunk):
+def read_block(ref, block, vectors, per_chunk, stride):
     part = math.gcd(vectors, per_chunk)
     pieces = []
     for row in range(block * vectors, (block + 1) * vectors, part):
-        at = row % per_chunk
-        pieces.append(ref[row // per_chunk, at : at + part, :])
+        at = row // per_chunk * stride + row % per_chunk
+        pieces.append(ref[at : at + part, :])
     return pieces[0] if len(pieces) == 1 else jnp.concatenate(pieces, axis=0)
 
 
-def write_block(ref, block, value, per_chunk):
+def write_block(ref, block, value, per_chunk, stride):
     vectors = value.shape[0]
     part = math.gcd(vectors, per_chunk)
     for begin in range(0, vectors, part):
         row = block * vectors + begin
-        at = row % per_chunk
-        ref[row // per_chunk, at : at + part, :] = value[begin : begin + part]
-
-
-def gram_panels(ref, per_chunk, vectors, count):
-    return [ref[c, per_chunk : per_chunk + SUB, :] * (1.0 / count) for c in range(vectors // SUB)]
+        at = row // per_chunk * stride + row % per_chunk
+        ref[at : at + part, :] = value[begin : begin + part]
+
+
+def pack(gram):
+    half = gram.shape[0] // 2
+    return jnp.concatenate([gram[:half], gram[half:]], axis=1)
+
+
+def unpacked_panels(packed):
+    vectors = packed.shape[1] // 2
+    turned = jnp.concatenate([packed[:, vectors:], packed[:, :vectors]], axis=1)
+    return [half[at : at + SUB] for half in (packed, turned) for at in range(0, vectors // 2, SUB)]
+
+
+def gram_panels(ref, chunks, per_chunk, vectors, count):
+    part = vectors // 2 // chunks
+    stride = per_chunk + part
+    rows = [ref[c * stride + per_chunk : (c + 1) * stride, :] for c in range(chunks)]
+    return unpacked_panels(jnp.concatenate(rows, axis=0) * (1.0 / count))
 
 
 def scale_of(degree):
     return lax.rsqrt(degree.astype(jnp.float32))
 
 
-def phase(data, degree, tiles, src, dst, used, blocks_out, out_chunks, forward, gram_count, send_gram, keep_raw):
+def phase(data, chunks, degree, tiles, src, dst, used, blocks_out, out_chunks, forward, gram_count, send_gram, keep_raw):
     slots, tile, _ = tiles.shape
     blocks = degree.shape[0]
-    begins = data.ndim == 2
+    begins = chunks is None
     vectors = data.shape[0] if begins else tile // 2
-    per_chunk = None if begins else blocks * vectors // data.shape[0]
+    per_chunk = None if begins else blocks * vectors // chunks
+    stride = None if begins else data.shape[0] // chunks
     have_gram = gram_count is not None
     terms = 1 if begins else 2
     out_per = blocks_out * vectors // out_chunks
-    out_rows = out_per + (SUB if send_gram else 0)
+    gram_rows = vectors // 2 // out_chunks if send_gram else 0
+    out_stride = out_per + gram_rows
     group_slots = BEGIN_GROUP if begins else GROUP
     dims = (((1,), (1,)), ((), ())) if forward else (((1,), (0,)), ((), ()))
 
@@ -138,7 +150,7 @@
     def product_phase(src_ref, dst_ref, used_ref, data_ref, degree_ref, tiles_ref, out_ref, raw_ref, x_ref, sums_ref, copy_of):
         sums_ref[...] = jnp.zeros_like(sums_ref)
         if have_gram:
-            inverse = inverse_factor(gram_panels(data_ref, per_chunk, vectors, gram_count))
+            inverse = inverse_factor(gram_panels(data_ref, chunks, per_chunk, vectors, gram_count))
         gram = jnp.zeros((vectors, vectors), jnp.float32)
         for first in range(0, blocks, WIDTH):
             group = range(first, first + WIDTH)
@@ -146,7 +158,7 @@
             if begins:
                 raw = data_ref[:, first * tile : (first + WIDTH) * tile]
             else:
-                raw = jnp.concatenate([read_block(data_ref, block, vectors, per_chunk) for block in group], axis=1)
+                raw = jnp.concatenate([read_block(data_ref, block, vectors, per_chunk, stride) for block in group], axis=1)
                 if have_gram:
                     raw = dot(inverse, raw)
                 raw = raw * weight
@@ -164,10 +176,10 @@
                 if keep_raw:
                     raw_ref[block] = raw[:, lanes]
         if send_gram:
-            both = padded(gram)
+            packed = pack(gram)
             for c in range(out_chunks):
-                inside = c * SUB < vectors
-                out_ref[c, out_per:, :] = both[c * SUB : (c + 1) * SUB] if inside else jnp.zeros((SUB, tile), jnp.float32)
+                at = c * out_stride + out_per
+                out_ref[at : at + gram_rows, :] = packed[c * gram_rows : (c + 1) * gram_rows]
 
         @pl.loop(0, slots // group_slots)
         def _(step):
@@ -183,9 +195,9 @@
                 sums_ref[jnp.where(at < used_ref[0], dst_ref[at], blocks_out)] += product
 
         for block in range(blocks_out):
-            write_block(out_ref, block, sums_ref[block], out_per)
-
-    out_shape = [jax.ShapeDtypeStruct((out_chunks, out_rows, tile), jnp.float32)]
+            write_block(out_ref, block, sums_ref[block], out_per, out_stride)
+
+    out_shape = [jax.ShapeDtypeStruct((out_chunks * out_stride, tile), jnp.float32)]
     if keep_raw:
         out_shape.append(jax.ShapeDtypeStruct((blocks, vectors, tile), jnp.float32))
     scratch = [
@@ -235,58 +247,64 @@
     )(*inputs)
 
 
-def total(ref, begin, end):
-    value = ref[0, begin:end, :]
-    for c in range(1, ref.shape[0]):
-        value = value + ref[c, begin:end, :]
-    return value
-
-
-def exchange(data, axis):
-    return lax.all_to_all(data, axis, 0, 0)
-
-
-def sum_copies(got, copies):
+def exchange(data, axis, count):
+    return lax.all_to_all(data.reshape(count, 1, -1), axis, 0, 0).reshape(data.shape)
+
+
+def sum_copies(got, count, copies, rows, stride):
+    step = got.shape[0] // count
+
     def body(got_ref, out_ref):
-        mine = total(got_ref, 0, got_ref.shape[1])
+        mine = got_ref[:rows, :]
+        for c in range(1, count):
+            mine = mine + got_ref[c * step : c * step + rows, :]
+        if stride > rows:
+            mine = jnp.concatenate([mine, jnp.zeros((stride - rows, mine.shape[1]), jnp.float32)], axis=0)
         for c in range(copies):
-            out_ref[c] = mine
-
-    return call(body, [got], [(copies,) + got.shape[1:]], "sum_copies")[0]
-
-
-def narrow_sum(chunks):
-    return exchange(sum_copies(exchange(chunks, "narrow"), chunks.shape[0]), "narrow")
-
-
-def wide_sum(chunks):
+            out_ref[c * stride : (c + 1) * stride, :] = mine
+
+    return call(body, [got], [(copies * stride, got.shape[1])], "sum_copies")[0]
+
+
+def narrow_sum(data):
+    count = lax.axis_size("narrow")
+    rows = data.shape[0] // count
+    return exchange(sum_copies(exchange(data, "narrow", count), count, count, rows, rows), "narrow", count)
+
+
+def wide_sum(data):
     near = ("y", "z_low")
-    part = sum_copies(exchange(chunks, near), lax.axis_size("z_high"))
-    return exchange(sum_copies(exchange(part, "z_high"), chunks.shape[0]), near)
-
-
-def finish_items(data, degree, user_count, copies):
-    chunks, _, tile = data.shape
+    near_count, far_count = lax.axis_size("y") * lax.axis_size("z_low"), lax.axis_size("z_high")
+    rows = data.shape[0] // near_count
+    stride = -(-rows // SUB) * SUB
+    part = sum_copies(exchange(data, near, near_count), near_count, far_count, rows, stride)
+    back = sum_copies(exchange(part, "z_high", far_count), far_count, near_count, rows, rows)
+    return exchange(back, near, near_count)
+
+
+def finish_items(data, chunks, degree, user_count, copies):
+    rows, tile = data.shape
     blocks = degree.shape[0]
     vectors = tile // 2
     per_chunk = blocks * vectors // chunks
+    stride = rows // chunks
 
     def body(data_ref, degree_ref, raw_ref, gram_ref, inverse_ref):
-        inverse = inverse_factor(gram_panels(data_ref, per_chunk, vectors, user_count))
+        inverse = inverse_factor(gram_panels(data_ref, chunks, per_chunk, vectors, user_count))
         inverse_ref[...] = inverse
         gram = jnp.zeros((vectors, vectors), jnp.float32)
         for first in range(0, blocks, WIDTH):
             group = range(first, first + WIDTH)
             weight = jnp.concatenate([scale_of(degree_ref[block]) for block in group], axis=1)
-            raw = jnp.concatenate([read_block(data_ref, block, vectors, per_chunk) for block in group], axis=1)
+            raw = jnp.concatenate([read_block(data_ref, block, vectors, per_chunk, stride) for block in group], axis=1)
             raw = dot(inverse, raw) * weight
             gram = gram + dot(raw, raw, last=True)
             raw_ref[:, first * tile : (first + WIDTH) * tile] = raw
-        packed = jnp.concatenate([gram[: vectors // 2], gram[vectors // 2 :]], axis=1)
+        packed = pack(gram)
         for c in range(copies):
-            gram_ref[c] = packed
-
-    shapes = [(vectors, blocks * tile), (copies, vectors // 2, tile), (vectors, vectors)]
+            gram_ref[c * vectors // 2 : (c + 1) * vectors // 2, :] = packed
+
+    shapes = [(vectors, blocks * tile), (copies * vectors // 2, tile), (vectors, vectors)]
     return call(body, [data, degree], shapes, "finish_items")
 
 
@@ -302,13 +320,14 @@
 
 def finish_vectors(raw, grams, item_count):
     vectors, rows = raw.shape
-    width = WIDTH * grams.shape[2]
+    half = vectors // 2
+    width = WIDTH * grams.shape[1]
 
     def body(raw_ref, grams_ref, out_ref):
-        gram = total(grams_ref, 0, vectors // 2) * (1.0 / item_count)
-        gram = jnp.concatenate([gram[:, :vectors], gram[:, vectors:]], axis=0)
-        gram = padded(gram)
-        inverse = inverse_factor([gram[at : at + SUB] for at in range(0, vectors, SUB)])
+        packed = grams_ref[:half, :]
+        for at in range(half, grams.shape[0], half):
+            packed = packed + grams_ref[at : at + half, :]
+        inverse = inverse_factor(unpacked_panels(packed * (1.0 / item_count)))
         for begin in range(0, rows, width):
             out_ref[:, begin : begin + width] = dot(inverse, raw_ref[:, begin : begin + width])
 
@@ -332,18 +351,18 @@
     for step in range(ITERS):
         first, last = step == 0, step == ITERS - 1
         (terms,) = phase(
-            item_data, items, tile_values, tile_col, tile_row, tile_count, user_blocks, narrow_count, True,
+            item_data, None if first else near_count, items, tile_values, tile_col, tile_row, tile_count, user_blocks, narrow_count, True,
             None if first else all_users, not first, False,
         )
         user_data = narrow_sum(terms)
         out = phase(
-            user_data, users, tile_values, tile_row, tile_col, tile_count, item_blocks, near_count, False,
+            user_data, narrow_count, users, tile_values, tile_row, tile_col, tile_count, item_blocks, near_count, False,
             None if first else all_items, True, last,
         )
         item_data = wide_sum(out[0])
     user_raw = out[1]
-    item_raw, grams, user_inverse = finish_items(item_data, items, all_users, narrow_count)
-    grams = exchange(grams, "narrow")
+    item_raw, grams, user_inverse = finish_items(item_data, near_count, items, all_users, narrow_count)
+    grams = exchange(grams, "narrow", narrow_count)
     user_vectors = finish_users(user_raw, user_inverse)
     item_vectors = finish_vectors(item_raw, grams, all_items)
     return (user_vectors, item_vectors)

time: 260 us -> 256 us (0.985)
  blocking collectives: 217 us -> 212 us
    all_to_all x10, blocking collectives: 217 us -> 212 us  [exchange(): lax.all_to_all(data.reshape(count, 1, -1), axis, 0, 0).reshape(data.shape)]
where the time goes in v7:
time: 256 us; the launch traced here: 255 us
  blocking collectives  212 us (83%)
  Pallas kernels  32.4 us (13%)
  starting transfers between devices  5.11 us (2%)
  waiting for transfers between devices  3.95 us (2%)
    all_to_all x10, blocking collectives, exchange(): lax.all_to_all(data.reshape(count, 1, -1), axis, 0, 0).reshape(data.shape)  212 us
    pallas_call x3, Pallas kernels, phase(): pl.pallas_call(body, in_specs=[SMEM] * 3 + [VMEM] * 3, out_specs=[VMEM] *...  15.4 us
    pallas_call x9, Pallas kernels, call(): pl.pallas_call(body, in_specs=[VMEM] * len(inputs), out_specs=[VMEM] * le...  9.4 us
    pallas_call x1, Pallas kernels, phase(): pl.pallas_call(body, grid_spec=pltpu.PrefetchScalarGridSpec(num_scalar_pr...  7.59 us
  transfers between devices with their start and end apart: 1, of which 1 were waited for; matrix products, arithmetic and copies ran while one was open for 0% of the time, Pallas kernels for 1%

profile of v7, /device:TPU:1, one launch (start us, length us, event | category | flops | bytes accessed | tf_op | source)
XLA Modules:
  0.0 255.3 jit_solution(10641516069159816105)
XLA Ops:
  1.3 0.0 copy-start
  1.3 0.0 copy-start.2
  1.3 0.0 copy-start.3
  1.3 0.0 copy-start.4
  1.3 7.6 %forward_begin.1 = f32[1024,128]{1,0:T(8,128)} custom-call(s32[128]{0:T(128)} %dst_ref.7, s32[128]{0:T(128)} %src_ref.7, s32[1]{0:T(128)S(6)} %copy.20.used_ref, f32[64,3072]{1,0:T(8,128)} %data_ref.1, s32[24,1,128]{2,1,0:T(1,128)} %bitcast.44, bf16[128,128,128]{2,1,0:T(8,128)(2,1)} %tiles_ref.7), custom_call_target="tpu_custom_call" | custom-call | tf_op jit(solution)/shard_map/forward_begin/pallas_call | solution.py:215
  8.9 23.3 %all_to_all.55 = f32[8,1,16384]{2,1,0:T(1,128)S(1)} all-to-all(f32[8,1,16384]{2,1,0:T(1,128)} %bitcast.49), channel_id=1, replica_groups=mesh['y'=8,'z_high'=6,'z_low'=2,'narrow'=8] {'narrow'}, dimensions={0} | all-to-all | bytes 1048576 | tf_op jit(solution)/shard_map/all_to_all | solution.py:251
  32.2 12.8 %all_to_all.56 = f32[8,1,16384]{2,1,0:T(1,128)S(1)} all-to-all(f32[8,1,16384]{2,1,0:T(1,128)S(1)} %bitcast.37), channel_id=1, replica_groups=mesh['y'=8,'z_high'=6,'z_low'=2,'narrow'=8] {'narrow'}, dimensions={0} | all-to-all | bytes 1048576 | tf_op jit(solution)/shard_map/all_to_all | solution.py:251
  45.0 0.0 copy-done
  45.1 0.0 copy-done.2
  45.1 0.0 copy-done.3
  45.1 0.0 copy-done.4
  45.1 2.8 %backward.2 = f32[1568,128]{1,0:T(8,128)S(1)} custom-call(s32[128]{0:T(128)S(1)} %copy-done.3, s32[128]{0:T(128)S(1)} %copy-done.4, s32[1]{0:T(128)S(6)} %copy.20.used_ref, f32[1024,128]{1,0:T(8,128)S(1)} %bitcast.35, s32[16,1,128]{2,1,0:T(1,128)S(1)} %bitcast.47, bf16[128,128,128]{2,1,0:T(8,128)(2,1)S(1)} %copy-done), custom_call_target="tpu_custom_call" | custom-call | tf_op jit(solution)/shard_map/backward/pallas_call | solution.py:228
  47.8 0.0 copy-start.1
  47.8 24.2 %all_to_all.57 = f32[16,1,12544]{2,1,0:T(1,128)S(1)} all-to-all(f32[16,1,12544]{2,1,0:T(1,128)S(1)} %bitcast.24), channel_id=1, replica_groups=mesh['y'=8,'z_high'=6,'z_low'=2,'narrow'=8] {'y','z_low'}, dimensions={0} | all-to-all | bytes 1605632 | tf_op jit(solution)/shard_map/all_to_all | solution.py:251
  72.0 0.1 sum_copies.7
  72.1 24.4 %all_to_all.58 = f32[6,1,13312]{2,1,0:T(1,128)S(1)} all-to-all(f32[6,1,13312]{2,1,0:T(1,128)S(1)} %bitcast.38), channel_id=1, replica_groups=mesh['y'=8,'z_high'=6,'z_low'=2,'narrow'=8] {'z_high'}, dimensions={0} | all-to-all | bytes 638976 | tf_op jit(solution)/shard_map/all_to_all | solution.py:251
  96.5 0.1 sum_copies.8
  96.5 28.7 %all_to_all.59 = f32[16,1,12544]{2,1,0:T(1,128)S(1)} all-to-all(f32[16,1,12544]{2,1,0:T(1,128)S(1)} %bitcast.27), channel_id=1, replica_groups=mesh['y'=8,'z_high'=6,'z_low'=2,'narrow'=8] {'y','z_low'}, dimensions={0} | all-to-all | bytes 1605632 | tf_op jit(solution)/shard_map/all_to_all | solution.py:251
  125.2 0.0 copy-done.1
  125.2 7.4 %forward.1 = f32[1056,128]{1,0:T(8,128)S(1)} custom-call(s32[128]{0:T(128)S(1)} %copy-done.4, s32[128]{0:T(128)S(1)} %copy-done.3, s32[1]{0:T(128)S(6)} %copy.20.used_ref, f32[1568,128]{1,0:T(8,128)S(1)} %bitcast.30, s32[24,1,128]{2,1,0:T(1,128)S(1)} %bitcast.45, bf16[128,128,128]{2,1,0:T(8,128)(2,1)S(1)} %copy-done), custom_call_target="tpu_custom_call" | custom-call | tf_op jit(solution)/shard_map/forward/pallas_call | solution.py:228
  132.6 14.3 %all_to_all.60 = f32[8,1,16896]{2,1,0:T(1,128)S(1)} all-to-all(f32[8,1,16896]{2,1,0:T(1,128)S(1)} %bitcast.34), channel_id=1, replica_groups=mesh['y'=8,'z_high'=6,'z_low'=2,'narrow'=8] {'narrow'}, dimensions={0} | all-to-all | bytes 1081344 | tf_op jit(solution)/shard_map/all_to_all | solution.py:251
  146.9 13.0 %all_to_all.61 = f32[8,1,16896]{2,1,0:T(1,128)S(1)} all-to-all(f32[8,1,16896]{2,1,0:T(1,128)S(1)} %bitcast.32), channel_id=1, replica_groups=mesh['y'=8,'z_high'=6,'z_low'=2,'narrow'=8] {'narrow'}, dimensions={0} | all-to-all | bytes 1081344 | tf_op jit(solution)/shard_map/all_to_all | solution.py:251
  159.9 5.3 %backward.3 = (f32[1568,128]{1,0:T(8,128)S(1)}, f32[16,64,128]{2,1,0:T(8,128)S(1)}) custom-call(s32[128]{0:T(128)S(1)} %copy-done.3, s32[128]{0:T(128)S(1)} %copy-done.4, s32[1]{0:T(128)S(6)} %copy.20.used_ref, f32[1056,128]{1,0:T(8,128)S(1)} %bitcast.33, s32[16,1,128]{2,1,0:T(1,128)S(1)} %bitcast.48, bf16[128,128,128]{2,1,0:T(8,128)(2,1)S(1)} %copy-done), custom_call_target="tpu_custom_call" | custom-call | tf_op jit(solution)/shard_map/backward/pallas_call | solution.py:228
  165.2 25.0 %all_to_all.62 = f32[16,1,12544]{2,1,0:T(1,128)S(1)} all-to-all(f32[16,1,12544]{2,1,0:T(1,128)S(1)} %bitcast.42), channel_id=1, replica_groups=mesh['y'=8,'z_high'=6,'z_low'=2,'narrow'=8] {'y','z_low'}, dimensions={0} | all-to-all | bytes 1605632 | tf_op jit(solution)/shard_map/all_to_all | solution.py:251
  190.2 0.1 sum_copies.10
  190.2 17.1 %all_to_all.63 = f32[6,1,13312]{2,1,0:T(1,128)S(1)} all-to-all(f32[6,1,13312]{2,1,0:T(1,128)S(1)} %bitcast.40), channel_id=1, replica_groups=mesh['y'=8,'z_high'=6,'z_low'=2,'narrow'=8] {'z_high'}, dimensions={0} | all-to-all | bytes 638976 | tf_op jit(solution)/shard_map/all_to_all | solution.py:251
  207.3 0.1 sum_copies.11
  207.4 29.8 %all_to_all.64 = f32[16,1,12544]{2,1,0:T(1,128)S(1)} all-to-all(f32[16,1,12544]{2,1,0:T(1,128)S(1)} %bitcast.29), channel_id=1, replica_groups=mesh['y'=8,'z_high'=6,'z_low'=2,'narrow'=8] {'y','z_low'}, dimensions={0} | all-to-all | bytes 1605632 | tf_op jit(solution)/shard_map/all_to_all | solution.py:251
  237.2 4.3 %finish_items.1 = (f32[64,3072]{1,0:T(8,128)S(1)}, f32[256,128]{1,0:T(8,128)}, f32[64,64]{1,0:T(8,128)S(1)}) custom-call(f32[1568,128]{1,0:T(8,128)S(1)} %bitcast.25, s32[24,1,128]{2,1,0:T(1,128)S(1)} %bitcast.46), custom_call_target="tpu_custom_call" | custom-call | tf_op jit(solution)/shard_map/finish_items/pallas_call | solution.py:240
  241.5 5.1 %all-to-all-start.10 = ((f32[8,1,4096]{2,1,0:T(1,128)}), f32[8,1,4096]{2,1,0:T(1,128)S(1)}, u32[]{:S(2)}, u32[]{:S(2)}) async-start(f32[8,1,4096]{2,1,0:T(1,128)} %bitcast.22), calls=%async_computation.10 | async-start | bytes 262144 | tf_op jit(solution)/shard_map/all_to_all | solution.py:251
  246.6 1.3 finish_users.1
  247.9 4.0 %all-to-all-done.10 = f32[8,1,4096]{2,1,0:T(1,128)S(1)} async-done(((f32[8,1,4096]{2,1,0:T(1,128)}), f32[8,1,4096]{2,1,0:T(1,128)S(1)}, u32[]{:S(2)}, u32[]{:S(2)}) %all-to-all-start.10) | async-done | bytes 131104 | tf_op jit(solution)/shard_map/all_to_all | solution.py:251
  251.9 3.4 %finish_vectors.1 = f32[64,3072]{1,0:T(8,128)} custom-call(f32[64,3072]{1,0:T(8,128)S(1)} %get-tuple-element.10.raw_ref, f32[256,128]{1,0:T(8,128)S(1)} %bitcast.43), custom_call_target="tpu_custom_call" | custom-call | tf_op jit(solution)/shard_map/finish_vectors/pallas_call | solution.py:240
  (2 shorter events, 0.1 us)
Async XLA Ops:
  1.3 43.8 %copy-start = (bf16[128,128,128]{2,1,0:T(8,128)(2,1)S(1)}, bf16[128,128,128]{2,1,0:T(8,128)(2,1)}, u32[]{:S(2)}) copy-start(bf16[128,128,128]{2,1,0:T(8,128)(2,1)} %tiles_ref.7) | copy-start | bytes 12582916
  1.3 43.8 %copy-start.2 = (s32[2048]{0:T(1024)S(1)}, s32[2048]{0:T(1024)}, u32[]{:S(2)}) copy-start(s32[2048]{0:T(1024)} %param.11) | copy-start | bytes 24580
  1.3 43.8 %copy-start.3 = (s32[128]{0:T(128)S(1)}, s32[128]{0:T(128)}, u32[]{:S(2)}) copy-start(s32[128]{0:T(128)} %src_ref.7) | copy-start | bytes 1540
  1.3 43.8 %copy-start.4 = (s32[128]{0:T(128)S(1)}, s32[128]{0:T(128)}, u32[]{:S(2)}) copy-start(s32[128]{0:T(128)} %dst_ref.7) | copy-start | bytes 1540
  47.8 77.4 %copy-start.1 = (s32[3072]{0:T(1024)S(1)}, s32[3072]{0:T(1024)}, u32[]{:S(2)}) copy-start(s32[3072]{0:T(1024)} %param.12) | copy-start | bytes 36868
  241.5 10.4 %all-to-all-start.10 = ((f32[8,1,4096]{2,1,0:T(1,128)}), f32[8,1,4096]{2,1,0:T(1,128)S(1)}, u32[]{:S(2)}, u32[]{:S(2)}) async-start(f32[8,1,4096]{2,1,0:T(1,128)} %bitcast.22), calls=%async_computation.10 | async-start | bytes 262144 | tf_op jit(solution)/shard_map/all_to_all | solution.py:251

commit v8 on v7

--- a/solution.py
+++ b/solution.py
@@ -8,7 +8,7 @@
 from jax.sharding import Mesh, PartitionSpec as P
 
 ITERS = 2
-GROUP = 64
+GROUP = 128
 BEGIN_GROUP = 32
 Y_CHIPS = 8
 Z_PAIR = 2

time: 256 us -> 254 us (level)
  no operation moved by 1% of the time
where the time goes in v8:
time: 254 us
  blocking collectives  213 us (84%)
  Pallas kernels  30.6 us (12%)
  starting transfers between devices  5.1 us (2%)
  waiting for transfers between devices  3.95 us (2%)
    all_to_all x10, blocking collectives, exchange(): lax.all_to_all(data.reshape(count, 1, -1), axis, 0, 0).reshape(data.shape)  213 us
    pallas_call x3, Pallas kernels, phase(): pl.pallas_call(body, in_specs=[SMEM] * 3 + [VMEM] * 3, out_specs=[VMEM] *...  13.7 us
    pallas_call x9, Pallas kernels, call(): pl.pallas_call(body, in_specs=[VMEM] * len(inputs), out_specs=[VMEM] * le...  9.4 us
    pallas_call x1, Pallas kernels, phase(): pl.pallas_call(body, grid_spec=pltpu.PrefetchScalarGridSpec(num_scalar_pr...  7.59 us
    all_to_all x1, starting transfers between devices, exchange(): lax.all_to_all(data.reshape(count, 1, -1), axis, 0, 0).reshape(data.shape)  5.1 us
  transfers between devices with their start and end apart: 1, of which 1 were waited for; matrix products, arithmetic and copies ran while one was open for 0% of the time, Pallas kernels for 1%

profile of v8, /device:TPU:1, one launch (start us, length us, event | category | flops | bytes accessed | tf_op | source)
XLA Modules:
  0.0 253.8 jit_solution(16051064621128771310)
XLA Ops:
  1.3 0.0 copy-start
  1.3 0.0 copy-start.2
  1.3 0.0 copy-start.3
  1.3 0.0 copy-start.4
  1.3 7.6 %forward_begin.1 = f32[1024,128]{1,0:T(8,128)} custom-call(s32[128]{0:T(128)} %dst_ref.7, s32[128]{0:T(128)} %src_ref.7, s32[1]{0:T(128)S(6)} %copy.20.used_ref, f32[64,3072]{1,0:T(8,128)} %data_ref.1, s32[24,1,128]{2,1,0:T(1,128)} %bitcast.44, bf16[128,128,128]{2,1,0:T(8,128)(2,1)} %tiles_ref.7), custom_call_target="tpu_custom_call" | custom-call | tf_op jit(solution)/shard_map/forward_begin/pallas_call | solution.py:215
  8.9 23.3 %all_to_all.55 = f32[8,1,16384]{2,1,0:T(1,128)S(1)} all-to-all(f32[8,1,16384]{2,1,0:T(1,128)} %bitcast.49), channel_id=1, replica_groups=mesh['y'=8,'z_high'=6,'z_low'=2,'narrow'=8] {'narrow'}, dimensions={0} | all-to-all | bytes 1048576 | tf_op jit(solution)/shard_map/all_to_all | solution.py:251
  32.2 12.8 %all_to_all.56 = f32[8,1,16384]{2,1,0:T(1,128)S(1)} all-to-all(f32[8,1,16384]{2,1,0:T(1,128)S(1)} %bitcast.37), channel_id=1, replica_groups=mesh['y'=8,'z_high'=6,'z_low'=2,'narrow'=8] {'narrow'}, dimensions={0} | all-to-all | bytes 1048576 | tf_op jit(solution)/shard_map/all_to_all | solution.py:251
  45.0 0.0 copy-done
  45.0 0.0 copy-done.2
  45.0 0.0 copy-done.3
  45.0 0.0 copy-done.4
  45.1 2.4 backward.2
  47.5 0.0 copy-start.1
  47.5 24.2 %all_to_all.57 = f32[16,1,12544]{2,1,0:T(1,128)S(1)} all-to-all(f32[16,1,12544]{2,1,0:T(1,128)S(1)} %bitcast.24), channel_id=1, replica_groups=mesh['y'=8,'z_high'=6,'z_low'=2,'narrow'=8] {'y','z_low'}, dimensions={0} | all-to-all | bytes 1605632 | tf_op jit(solution)/shard_map/all_to_all | solution.py:251
  71.7 0.1 sum_copies.7
  71.7 24.4 %all_to_all.58 = f32[6,1,13312]{2,1,0:T(1,128)S(1)} all-to-all(f32[6,1,13312]{2,1,0:T(1,128)S(1)} %bitcast.38), channel_id=1, replica_groups=mesh['y'=8,'z_high'=6,'z_low'=2,'narrow'=8] {'z_high'}, dimensions={0} | all-to-all | bytes 638976 | tf_op jit(solution)/shard_map/all_to_all | solution.py:251
  96.2 0.1 sum_copies.8
  96.2 28.7 %all_to_all.59 = f32[16,1,12544]{2,1,0:T(1,128)S(1)} all-to-all(f32[16,1,12544]{2,1,0:T(1,128)S(1)} %bitcast.27), channel_id=1, replica_groups=mesh['y'=8,'z_high'=6,'z_low'=2,'narrow'=8] {'y','z_low'}, dimensions={0} | all-to-all | bytes 1605632 | tf_op jit(solution)/shard_map/all_to_all | solution.py:251
  124.9 0.0 copy-done.1
  124.9 6.6 %forward.1 = f32[1056,128]{1,0:T(8,128)S(1)} custom-call(s32[128]{0:T(128)S(1)} %copy-done.4, s32[128]{0:T(128)S(1)} %copy-done.3, s32[1]{0:T(128)S(6)} %copy.20.used_ref, f32[1568,128]{1,0:T(8,128)S(1)} %bitcast.30, s32[24,1,128]{2,1,0:T(1,128)S(1)} %bitcast.45, bf16[128,128,128]{2,1,0:T(8,128)(2,1)S(1)} %copy-done), custom_call_target="tpu_custom_call" | custom-call | tf_op jit(solution)/shard_map/forward/pallas_call | solution.py:228
  131.5 14.2 %all_to_all.60 = f32[8,1,16896]{2,1,0:T(1,128)S(1)} all-to-all(f32[8,1,16896]{2,1,0:T(1,128)S(1)} %bitcast.34), channel_id=1, replica_groups=mesh['y'=8,'z_high'=6,'z_low'=2,'narrow'=8] {'narrow'}, dimensions={0} | all-to-all | bytes 1081344 | tf_op jit(solution)/shard_map/all_to_all | solution.py:251
  145.8 13.0 %all_to_all.61 = f32[8,1,16896]{2,1,0:T(1,128)S(1)} all-to-all(f32[8,1,16896]{2,1,0:T(1,128)S(1)} %bitcast.32), channel_id=1, replica_groups=mesh['y'=8,'z_high'=6,'z_low'=2,'narrow'=8] {'narrow'}, dimensions={0} | all-to-all | bytes 1081344 | tf_op jit(solution)/shard_map/all_to_all | solution.py:251
  158.8 4.6 %backward.3 = (f32[1568,128]{1,0:T(8,128)S(1)}, f32[16,64,128]{2,1,0:T(8,128)S(1)}) custom-call(s32[128]{0:T(128)S(1)} %copy-done.3, s32[128]{0:T(128)S(1)} %copy-done.4, s32[1]{0:T(128)S(6)} %copy.20.used_ref, f32[1056,128]{1,0:T(8,128)S(1)} %bitcast.33, s32[16,1,128]{2,1,0:T(1,128)S(1)} %bitcast.48, bf16[128,128,128]{2,1,0:T(8,128)(2,1)S(1)} %copy-done), custom_call_target="tpu_custom_call" | custom-call | tf_op jit(solution)/shard_map/backward/pallas_call | solution.py:228
  163.5 25.2 %all_to_all.62 = f32[16,1,12544]{2,1,0:T(1,128)S(1)} all-to-all(f32[16,1,12544]{2,1,0:T(1,128)S(1)} %bitcast.42), channel_id=1, replica_groups=mesh['y'=8,'z_high'=6,'z_low'=2,'narrow'=8] {'y','z_low'}, dimensions={0} | all-to-all | bytes 1605632 | tf_op jit(solution)/shard_map/all_to_all | solution.py:251
  188.6 0.1 sum_copies.10
  188.7 17.1 %all_to_all.63 = f32[6,1,13312]{2,1,0:T(1,128)S(1)} all-to-all(f32[6,1,13312]{2,1,0:T(1,128)S(1)} %bitcast.40), channel_id=1, replica_groups=mesh['y'=8,'z_high'=6,'z_low'=2,'narrow'=8] {'z_high'}, dimensions={0} | all-to-all | bytes 638976 | tf_op jit(solution)/shard_map/all_to_all | solution.py:251
  205.7 0.1 sum_copies.11
  205.8 29.8 %all_to_all.64 = f32[16,1,12544]{2,1,0:T(1,128)S(1)} all-to-all(f32[16,1,12544]{2,1,0:T(1,128)S(1)} %bitcast.29), channel_id=1, replica_groups=mesh['y'=8,'z_high'=6,'z_low'=2,'narrow'=8] {'y','z_low'}, dimensions={0} | all-to-all | bytes 1605632 | tf_op jit(solution)/shard_map/all_to_all | solution.py:251
  235.6 4.3 %finish_items.1 = (f32[64,3072]{1,0:T(8,128)S(1)}, f32[256,128]{1,0:T(8,128)}, f32[64,64]{1,0:T(8,128)S(1)}) custom-call(f32[1568,128]{1,0:T(8,128)S(1)} %bitcast.25, s32[24,1,128]{2,1,0:T(1,128)S(1)} %bitcast.46), custom_call_target="tpu_custom_call" | custom-call | tf_op jit(solution)/shard_map/finish_items/pallas_call | solution.py:240
  239.9 5.1 %all-to-all-start.10 = ((f32[8,1,4096]{2,1,0:T(1,128)}), f32[8,1,4096]{2,1,0:T(1,128)S(1)}, u32[]{:S(2)}, u32[]{:S(2)}) async-start(f32[8,1,4096]{2,1,0:T(1,128)} %bitcast.22), calls=%async_computation.10 | async-start | bytes 262144 | tf_op jit(solution)/shard_map/all_to_all | solution.py:251
  245.0 1.3 finish_users.1
  246.4 4.0 %all-to-all-done.10 = f32[8,1,4096]{2,1,0:T(1,128)S(1)} async-done(((f32[8,1,4096]{2,1,0:T(1,128)}), f32[8,1,4096]{2,1,0:T(1,128)S(1)}, u32[]{:S(2)}, u32[]{:S(2)}) %all-to-all-start.10) | async-done | bytes 131104 | tf_op jit(solution)/shard_map/all_to_all | solution.py:251
  250.3 3.4 %finish_vectors.1 = f32[64,3072]{1,0:T(8,128)} custom-call(f32[64,3072]{1,0:T(8,128)S(1)} %get-tuple-element.10.raw_ref, f32[256,128]{1,0:T(8,128)S(1)} %bitcast.43), custom_call_target="tpu_custom_call" | custom-call | tf_op jit(solution)/shard_map/finish_vectors/pallas_call | solution.py:240
  (2 shorter events, 0.1 us)
Async XLA Ops:
  1.3 43.8 %copy-start = (bf16[128,128,128]{2,1,0:T(8,128)(2,1)S(1)}, bf16[128,128,128]{2,1,0:T(8,128)(2,1)}, u32[]{:S(2)}) copy-start(bf16[128,128,128]{2,1,0:T(8,128)(2,1)} %tiles_ref.7) | copy-start | bytes 12582916
  1.3 43.8 %copy-start.2 = (s32[2048]{0:T(1024)S(1)}, s32[2048]{0:T(1024)}, u32[]{:S(2)}) copy-start(s32[2048]{0:T(1024)} %param.11) | copy-start | bytes 24580
  1.3 43.7 %copy-start.3 = (s32[128]{0:T(128)S(1)}, s32[128]{0:T(128)}, u32[]{:S(2)}) copy-start(s32[128]{0:T(128)} %src_ref.7) | copy-start | bytes 1540
  1.3 43.7 %copy-start.4 = (s32[128]{0:T(128)S(1)}, s32[128]{0:T(128)}, u32[]{:S(2)}) copy-start(s32[128]{0:T(128)} %dst_ref.7) | copy-start | bytes 1540
  47.5 77.4 %copy-start.1 = (s32[3072]{0:T(1024)S(1)}, s32[3072]{0:T(1024)}, u32[]{:S(2)}) copy-start(s32[3072]{0:T(1024)} %param.12) | copy-start | bytes 36868
  239.9 10.4 %all-to-all-start.10 = ((f32[8,1,4096]{2,1,0:T(1,128)}), f32[8,1,4096]{2,1,0:T(1,128)S(1)}, u32[]{:S(2)}, u32[]{:S(2)}) async-start(f32[8,1,4096]{2,1,0:T(1,128)} %bitcast.22), calls=%async_computation.10 | async-start | bytes 262144 | tf_op jit(solution)/shard_map/all_to_all | solution.py:251

commit v9 on v8

--- a/solution.py
+++ b/solution.py
@@ -9,7 +9,7 @@
 
 ITERS = 2
 GROUP = 128
-BEGIN_GROUP = 32
+BEGIN_GROUP = 64
 Y_CHIPS = 8
 Z_PAIR = 2
 SUB = 8

time: 254 us -> 254 us (level)
  no operation moved by 1% of the time
where the time goes in v9:
time: 254 us; the launch traced here: 253 us
  blocking collectives  213 us (84%)
  Pallas kernels  30.1 us (12%)
  starting transfers between devices  5.1 us (2%)
  waiting for transfers between devices  3.95 us (2%)
    all_to_all x10, blocking collectives, exchange(): lax.all_to_all(data.reshape(count, 1, -1), axis, 0, 0).reshape(data.shape)  213 us
    pallas_call x3, Pallas kernels, phase(): pl.pallas_call(body, in_specs=[SMEM] * 3 + [VMEM] * 3, out_specs=[VMEM] *...  13.7 us
    pallas_call x9, Pallas kernels, call(): pl.pallas_call(body, in_specs=[VMEM] * len(inputs), out_specs=[VMEM] * le...  9.4 us
    pallas_call x1, Pallas kernels, phase(): pl.pallas_call(body, grid_spec=pltpu.PrefetchScalarGridSpec(num_scalar_pr...  7.04 us
    all_to_all x1, starting transfers between devices, exchange(): lax.all_to_all(data.reshape(count, 1, -1), axis, 0, 0).reshape(data.shape)  5.1 us
  transfers between devices with their start and end apart: 1, of which 1 were waited for; matrix products, arithmetic and copies ran while one was open for 0% of the time, Pallas kernels for 1%

profile of v9, /device:TPU:1, one launch (start us, length us, event | category | flops | bytes accessed | tf_op | source)
XLA Modules:
  0.0 253.1 jit_solution(17505791764297911701)
XLA Ops:
  1.3 0.0 copy-start
  1.3 0.0 copy-start.2
  1.3 0.0 copy-start.3
  1.3 0.0 copy-start.4
  1.3 7.0 %forward_begin.1 = f32[1024,128]{1,0:T(8,128)} custom-call(s32[128]{0:T(128)} %dst_ref.7, s32[128]{0:T(128)} %src_ref.7, s32[1]{0:T(128)S(6)} %copy.20.used_ref, f32[64,3072]{1,0:T(8,128)} %data_ref.1, s32[24,1,128]{2,1,0:T(1,128)} %bitcast.44, bf16[128,128,128]{2,1,0:T(8,128)(2,1)} %tiles_ref.7), custom_call_target="tpu_custom_call" | custom-call | tf_op jit(solution)/shard_map/forward_begin/pallas_call | solution.py:215
  8.4 23.3 %all_to_all.55 = f32[8,1,16384]{2,1,0:T(1,128)S(1)} all-to-all(f32[8,1,16384]{2,1,0:T(1,128)} %bitcast.49), channel_id=1, replica_groups=mesh['y'=8,'z_high'=6,'z_low'=2,'narrow'=8] {'narrow'}, dimensions={0} | all-to-all | bytes 1048576 | tf_op jit(solution)/shard_map/all_to_all | solution.py:251
  31.7 12.8 %all_to_all.56 = f32[8,1,16384]{2,1,0:T(1,128)S(1)} all-to-all(f32[8,1,16384]{2,1,0:T(1,128)S(1)} %bitcast.37), channel_id=1, replica_groups=mesh['y'=8,'z_high'=6,'z_low'=2,'narrow'=8] {'narrow'}, dimensions={0} | all-to-all | bytes 1048576 | tf_op jit(solution)/shard_map/all_to_all | solution.py:251
  44.5 0.0 copy-done
  44.5 0.0 copy-done.2
  44.5 0.0 copy-done.3
  44.5 0.0 copy-done.4
  44.5 2.4 backward.2
  46.9 0.0 copy-start.1
  47.0 24.2 %all_to_all.57 = f32[16,1,12544]{2,1,0:T(1,128)S(1)} all-to-all(f32[16,1,12544]{2,1,0:T(1,128)S(1)} %bitcast.24), channel_id=1, replica_groups=mesh['y'=8,'z_high'=6,'z_low'=2,'narrow'=8] {'y','z_low'}, dimensions={0} | all-to-all | bytes 1605632 | tf_op jit(solution)/shard_map/all_to_all | solution.py:251
  71.2 0.1 sum_copies.7
  71.2 24.4 %all_to_all.58 = f32[6,1,13312]{2,1,0:T(1,128)S(1)} all-to-all(f32[6,1,13312]{2,1,0:T(1,128)S(1)} %bitcast.38), channel_id=1, replica_groups=mesh['y'=8,'z_high'=6,'z_low'=2,'narrow'=8] {'z_high'}, dimensions={0} | all-to-all | bytes 638976 | tf_op jit(solution)/shard_map/all_to_all | solution.py:251
  95.6 0.1 sum_copies.8
  95.7 28.6 %all_to_all.59 = f32[16,1,12544]{2,1,0:T(1,128)S(1)} all-to-all(f32[16,1,12544]{2,1,0:T(1,128)S(1)} %bitcast.27), channel_id=1, replica_groups=mesh['y'=8,'z_high'=6,'z_low'=2,'narrow'=8] {'y','z_low'}, dimensions={0} | all-to-all | bytes 1605632 | tf_op jit(solution)/shard_map/all_to_all | solution.py:251
  124.3 0.0 copy-done.1
  124.3 6.6 %forward.1 = f32[1056,128]{1,0:T(8,128)S(1)} custom-call(s32[128]{0:T(128)S(1)} %copy-done.4, s32[128]{0:T(128)S(1)} %copy-done.3, s32[1]{0:T(128)S(6)} %copy.20.used_ref, f32[1568,128]{1,0:T(8,128)S(1)} %bitcast.30, s32[24,1,128]{2,1,0:T(1,128)S(1)} %bitcast.45, bf16[128,128,128]{2,1,0:T(8,128)(2,1)S(1)} %copy-done), custom_call_target="tpu_custom_call" | custom-call | tf_op jit(solution)/shard_map/forward/pallas_call | solution.py:228
  130.9 14.4 %all_to_all.60 = f32[8,1,16896]{2,1,0:T(1,128)S(1)} all-to-all(f32[8,1,16896]{2,1,0:T(1,128)S(1)} %bitcast.34), channel_id=1, replica_groups=mesh['y'=8,'z_high'=6,'z_low'=2,'narrow'=8] {'narrow'}, dimensions={0} | all-to-all | bytes 1081344 | tf_op jit(solution)/shard_map/all_to_all | solution.py:251
  145.3 13.0 %all_to_all.61 = f32[8,1,16896]{2,1,0:T(1,128)S(1)} all-to-all(f32[8,1,16896]{2,1,0:T(1,128)S(1)} %bitcast.32), channel_id=1, replica_groups=mesh['y'=8,'z_high'=6,'z_low'=2,'narrow'=8] {'narrow'}, dimensions={0} | all-to-all | bytes 1081344 | tf_op jit(solution)/shard_map/all_to_all | solution.py:251
  158.3 4.6 %backward.3 = (f32[1568,128]{1,0:T(8,128)S(1)}, f32[16,64,128]{2,1,0:T(8,128)S(1)}) custom-call(s32[128]{0:T(128)S(1)} %copy-done.3, s32[128]{0:T(128)S(1)} %copy-done.4, s32[1]{0:T(128)S(6)} %copy.20.used_ref, f32[1056,128]{1,0:T(8,128)S(1)} %bitcast.33, s32[16,1,128]{2,1,0:T(1,128)S(1)} %bitcast.48, bf16[128,128,128]{2,1,0:T(8,128)(2,1)S(1)} %copy-done), custom_call_target="tpu_custom_call" | custom-call | tf_op jit(solution)/shard_map/backward/pallas_call | solution.py:228
  162.9 24.9 %all_to_all.62 = f32[16,1,12544]{2,1,0:T(1,128)S(1)} all-to-all(f32[16,1,12544]{2,1,0:T(1,128)S(1)} %bitcast.42), channel_id=1, replica_groups=mesh['y'=8,'z_high'=6,'z_low'=2,'narrow'=8] {'y','z_low'}, dimensions={0} | all-to-all | bytes 1605632 | tf_op jit(solution)/shard_map/all_to_all | solution.py:251
  187.8 0.1 sum_copies.10
  187.9 17.1 %all_to_all.63 = f32[6,1,13312]{2,1,0:T(1,128)S(1)} all-to-all(f32[6,1,13312]{2,1,0:T(1,128)S(1)} %bitcast.40), channel_id=1, replica_groups=mesh['y'=8,'z_high'=6,'z_low'=2,'narrow'=8] {'z_high'}, dimensions={0} | all-to-all | bytes 638976 | tf_op jit(solution)/shard_map/all_to_all | solution.py:251
  205.0 0.1 sum_copies.11
  205.1 29.8 %all_to_all.64 = f32[16,1,12544]{2,1,0:T(1,128)S(1)} all-to-all(f32[16,1,12544]{2,1,0:T(1,128)S(1)} %bitcast.29), channel_id=1, replica_groups=mesh['y'=8,'z_high'=6,'z_low'=2,'narrow'=8] {'y','z_low'}, dimensions={0} | all-to-all | bytes 1605632 | tf_op jit(solution)/shard_map/all_to_all | solution.py:251
  234.9 4.3 %finish_items.1 = (f32[64,3072]{1,0:T(8,128)S(1)}, f32[256,128]{1,0:T(8,128)}, f32[64,64]{1,0:T(8,128)S(1)}) custom-call(f32[1568,128]{1,0:T(8,128)S(1)} %bitcast.25, s32[24,1,128]{2,1,0:T(1,128)S(1)} %bitcast.46), custom_call_target="tpu_custom_call" | custom-call | tf_op jit(solution)/shard_map/finish_items/pallas_call | solution.py:240
  239.2 5.1 %all-to-all-start.10 = ((f32[8,1,4096]{2,1,0:T(1,128)}), f32[8,1,4096]{2,1,0:T(1,128)S(1)}, u32[]{:S(2)}, u32[]{:S(2)}) async-start(f32[8,1,4096]{2,1,0:T(1,128)} %bitcast.22), calls=%async_computation.10 | async-start | bytes 262144 | tf_op jit(solution)/shard_map/all_to_all | solution.py:251
  244.3 1.3 finish_users.1
  245.7 4.0 %all-to-all-done.10 = f32[8,1,4096]{2,1,0:T(1,128)S(1)} async-done(((f32[8,1,4096]{2,1,0:T(1,128)}), f32[8,1,4096]{2,1,0:T(1,128)S(1)}, u32[]{:S(2)}, u32[]{:S(2)}) %all-to-all-start.10) | async-done | bytes 131104 | tf_op jit(solution)/shard_map/all_to_all | solution.py:251
  249.6 3.4 %finish_vectors.1 = f32[64,3072]{1,0:T(8,128)} custom-call(f32[64,3072]{1,0:T(8,128)S(1)} %get-tuple-element.10.raw_ref, f32[256,128]{1,0:T(8,128)S(1)} %bitcast.43), custom_call_target="tpu_custom_call" | custom-call | tf_op jit(solution)/shard_map/finish_vectors/pallas_call | solution.py:240
  (2 shorter events, 0.1 us)
Async XLA Ops:
  1.3 43.2 %copy-start = (bf16[128,128,128]{2,1,0:T(8,128)(2,1)S(1)}, bf16[128,128,128]{2,1,0:T(8,128)(2,1)}, u32[]{:S(2)}) copy-start(bf16[128,128,128]{2,1,0:T(8,128)(2,1)} %tiles_ref.7) | copy-start | bytes 12582916
  1.3 43.2 %copy-start.2 = (s32[2048]{0:T(1024)S(1)}, s32[2048]{0:T(1024)}, u32[]{:S(2)}) copy-start(s32[2048]{0:T(1024)} %param.11) | copy-start | bytes 24580
  1.3 43.2 %copy-start.3 = (s32[128]{0:T(128)S(1)}, s32[128]{0:T(128)}, u32[]{:S(2)}) copy-start(s32[128]{0:T(128)} %src_ref.7) | copy-start | bytes 1540
  1.3 43.2 %copy-start.4 = (s32[128]{0:T(128)S(1)}, s32[128]{0:T(128)}, u32[]{:S(2)}) copy-start(s32[128]{0:T(128)} %dst_ref.7) | copy-start | bytes 1540
  46.9 77.3 %copy-start.1 = (s32[3072]{0:T(1024)S(1)}, s32[3072]{0:T(1024)}, u32[]{:S(2)}) copy-start(s32[3072]{0:T(1024)} %param.12) | copy-start | bytes 36868
  239.2 10.4 %all-to-all-start.10 = ((f32[8,1,4096]{2,1,0:T(1,128)}), f32[8,1,4096]{2,1,0:T(1,128)S(1)}, u32[]{:S(2)}, u32[]{:S(2)}) async-start(f32[8,1,4096]{2,1,0:T(1,128)} %bitcast.22), calls=%async_computation.10 | async-start | bytes 262144 | tf_op jit(solution)/shard_map/all_to_all | solution.py:251
